TPU v7x, 256 devices: a whole 4x4x8 slice. The times are simulated.
256 devices in a mesh: dp: 64 (over y, z, core), seq: 4 (over x).
Axes of the slice: x: 4, y: 4, z: 8, core: 2. Of those that a mesh axis runs over, the one named last changes fastest.
Arguments:
- audio: bfloat16 [192, 100, 1280], P('dp', None, 'seq'), may hold values from -10 to 10
- counts: int32 [64], P('dp'), may hold values from 1 to 3, as said below
- lengths: int32 [192], P('dp'), may hold values from 2 to 100, as said below
- positions: int32 [192, 50], P('dp'), may hold values from 0 to 159, as said below
- w_qkv: bfloat16 [3, 1280, 1280], P(None, None, 'seq'), may hold values from -8 to 8
- w_out: bfloat16 [1280, 1280], P('seq'), may hold values from -0.15625 to 0.15625
- w_proj: bfloat16 [1280, 3584], P(None, 'seq'), may hold values from -0.15625 to 0.15625
- cotangent: bfloat16 [10240, 3584], P(('dp', 'seq')), may hold values from -0.0625 to 0.0625
Outputs:
- embeds: bfloat16 [10240, 3584], P(('dp', 'seq'))
- grad_qkv: float32 [3, 1280, 1280], P(None, 'dp', 'seq')
- grad_out: float32 [1280, 1280], P('seq', 'dp')
Inputs may be any that keep to these rules, and one draw needn't show every extreme that they name: `counts`: for i below 32, entries i and i + 32 sum to at most 4. `lengths`: even. `positions`: the 150 entries of the blocks of one index of dp all differ.
All inputs are finite; a program needn't handle non-finite values.
Results may differ from a plain program's by a relative error of at most 0.023.
Values may be sent and summed in bfloat16 or wider, within the bound.
A program may use at most 128 MiB of HBM per device.

v0:
```python
import jax
import jax.numpy as jnp
from jax import lax
from jax.sharding import PartitionSpec as P

HS = 64


EPSILON = 1e-05


def normalize(row_block):
    average = jnp.mean(row_block, axis=-1, keepdims=True)
    centred = row_block - average
    spread = jnp.mean(centred * centred, axis=-1, keepdims=True)
    inverse = lax.rsqrt(spread + EPSILON)
    return (centred * inverse, inverse)


def attend_forward(queries, keys_in, values_in, key_ok, scaling):
    scores = (
        jnp.einsum("bqhd,bkhd->bhqk", queries, keys_in, preferred_element_type=jnp.float32)
        * scaling
    )
    scores = jnp.where(key_ok[:, None, None, :], scores, jnp.float32(-1e30))
    row_top = jnp.max(scores, axis=-1, keepdims=True)
    powered = jnp.exp(scores - row_top)
    weights = powered / jnp.sum(powered, axis=-1, keepdims=True)
    weights_half = weights.astype(jnp.bfloat16)
    attended = jnp.einsum(
        "bhqk,bkhd->bqhd", weights_half, values_in, preferred_element_type=jnp.float32
    )
    return (weights, weights_half, attended.astype(jnp.bfloat16))


def attend_backward(queries, keys_in, values_in, weights, weights_half, mixed_grad, scaling):
    prob_grad = jnp.einsum(
        "bqhd,bkhd->bhqk", mixed_grad, values_in, preferred_element_type=jnp.float32
    )
    score_grad = weights * (prob_grad - jnp.sum(weights * prob_grad, axis=-1, keepdims=True))
    score_half = score_grad.astype(jnp.bfloat16)
    query_grad = (
        jnp.einsum("bhqk,bkhd->bqhd", score_half, keys_in, preferred_element_type=jnp.float32)
        * scaling
    )
    key_grad = (
        jnp.einsum("bhqk,bqhd->bkhd", score_half, queries, preferred_element_type=jnp.float32)
        * scaling
    )
    value_grad = jnp.einsum(
        "bhqk,bqhd->bkhd", weights_half, mixed_grad, preferred_element_type=jnp.float32
    )
    return (
        query_grad.astype(jnp.bfloat16),
        key_grad.astype(jnp.bfloat16),
        value_grad.astype(jnp.bfloat16),
    )


def shards(audio, counts, lengths, positions, w_qkv, w_out, w_proj, cotangent):
    slot_count = audio.shape[0]
    frames = audio.shape[1]
    share_width = audio.shape[2]
    seq_size = lax.axis_size("seq")
    model_width = share_width * seq_size
    pooled_frames = frames // 2
    head_count = share_width // HS
    scaling = HS ** (-0.5)
    block_count = counts[0]
    slot_index = jnp.arange(slot_count, dtype=jnp.int32)
    live_length = jnp.where(slot_index < block_count, lengths, 0)
    work_blocks = audio.shape[0]
    row_total = work_blocks * frames
    full_audio = lax.all_gather(audio, "seq", axis=2, tiled=True)
    normed_half = (
        normalize(full_audio.astype(jnp.float32))[0]
        .astype(jnp.bfloat16)
        .reshape(row_total, model_width)
    )
    projected = jnp.einsum(
        "rd,jde->jre", normed_half, w_qkv, preferred_element_type=jnp.float32
    ).astype(jnp.bfloat16)
    shaped = projected.reshape(3, work_blocks, frames, head_count, HS)
    queries = shaped[0]
    keys_in = shaped[1]
    values_in = shaped[2]
    key_ok = jnp.arange(frames, dtype=jnp.int32)[None, :] < jnp.maximum(live_length, 1)[:, None]
    weights, weights_half, attended = attend_forward(queries, keys_in, values_in, key_ok, scaling)
    attended_rows = attended.reshape(row_total, share_width)
    head_terms = jnp.dot(attended_rows, w_out, preferred_element_type=jnp.float32)
    attention = lax.psum(head_terms.astype(jnp.bfloat16), "seq").astype(jnp.float32)
    hidden = full_audio.reshape(row_total, model_width).astype(jnp.float32) + attention
    pooled = jnp.mean(hidden.reshape(work_blocks, pooled_frames, 2, model_width), axis=2)
    normed_rows, inverse = normalize(pooled)
    send_rows = normed_rows.astype(jnp.bfloat16)
    owner_flat = send_rows.reshape(slot_count * pooled_frames, model_width)
    row_live = (
        jnp.arange(pooled_frames, dtype=jnp.int32)[None, :] < (live_length // 2)[:, None]
    ).reshape(-1, 1)
    target = positions.reshape(-1)
    adapter_rows = jnp.dot(owner_flat, w_proj, preferred_element_type=jnp.float32).astype(
        jnp.bfloat16
    )
    placed = jnp.where(row_live, adapter_rows, jnp.zeros_like(adapter_rows))
    slot_table = (
        jnp.zeros((cotangent.shape[0] * seq_size, w_proj.shape[1]), jnp.bfloat16)
        .at[target]
        .set(placed)
    )
    embeds = lax.all_to_all(slot_table, "seq", split_axis=0, concat_axis=1, tiled=True)
    column_grads = lax.all_to_all(cotangent, "seq", split_axis=1, concat_axis=0, tiled=True)
    row_grads = jnp.where(row_live, column_grads[target], jnp.zeros_like(adapter_rows))
    adapter_terms = lax.dot_general(
        row_grads, w_proj, (((1,), (1,)), ((), ())), preferred_element_type=jnp.float32
    )
    adapter_terms = adapter_terms.reshape(slot_count, pooled_frames, model_width)
    adapted_grad = lax.psum_scatter(
        adapter_terms.astype(jnp.bfloat16), "seq", scatter_dimension=2, tiled=True
    )
    grad_full = lax.all_gather(adapted_grad, "seq", axis=2, tiled=True).astype(jnp.float32)
    pooled_grad = inverse * (
        grad_full
        - jnp.mean(grad_full, axis=-1, keepdims=True)
        - normed_rows * jnp.mean(grad_full * normed_rows, axis=-1, keepdims=True)
    )
    attention_grad = (
        jnp.repeat(pooled_grad * 0.5, 2, axis=1)
        .astype(jnp.bfloat16)
        .reshape(row_total, model_width)
    )
    out_term = lax.dot_general(
        attended_rows, attention_grad, (((0,), (0,)), ((), ())), preferred_element_type=jnp.float32
    )
    mixed_grad = lax.dot_general(
        attention_grad, w_out, (((1,), (1,)), ((), ())), preferred_element_type=jnp.float32
    )
    mixed_grad = mixed_grad.astype(jnp.bfloat16).reshape(work_blocks, frames, head_count, HS)
    query_grad, key_grad, value_grad = attend_backward(
        queries, keys_in, values_in, weights, weights_half, mixed_grad, scaling
    )
    stacked = jnp.stack([query_grad, key_grad, value_grad]).reshape(3, row_total, share_width)
    qkv_term = jnp.einsum("rd,jre->jde", normed_half, stacked, preferred_element_type=jnp.float32)
    grad_qkv, grad_out = (
        lax.psum_scatter(qkv_term, "dp", scatter_dimension=1, tiled=True),
        lax.psum_scatter(out_term, "dp", scatter_dimension=1, tiled=True),
    )
    return (embeds, grad_qkv, grad_out)


def solution(mesh):
    in_specs = (
        P("dp", None, "seq"),
        P("dp"),
        P("dp"),
        P("dp", None),
        P(None, None, "seq"),
        P("seq", None),
        P(None, "seq"),
        P(("dp", "seq"), None),
    )
    out_specs = (P(("dp", "seq"), None), P(None, "dp", "seq"), P("seq", "dp"))
    return jax.shard_map(shards, mesh=mesh, in_specs=in_specs, out_specs=out_specs, check_vma=False)
```

profile of v0, /device:TPU:1, one launch (start us, length us, event | category | flops | bytes accessed | tf_op | source)
XLA Modules:
  0.0 425.0 jit_solution(4953501293739802707)
XLA Ops:
  9.0 4.8 %all-to-all-start.1 = ((bf16[40,4,896]{2,0,1:T(8,128)(2,1)}), bf16[40,4,896]{2,0,1:T(8,128)(2,1)S(1)}, u32[]{:S(2)}, u32[]{:S(2)}) async-start(bf16[40,4,896]{2,0,1:T(8,128)(2,1)} %bitcast.54), calls=%async_computation.1 | async-start | bytes 573440 | tf_op jit(solution)/shard_map/all_to_all | solution.py:111
  15.7 15.3 %all_gather.6 = bf16[3,100,1280]{1,0,2:T(4,128)(2,1)S(1)} all-gather(bf16[3,100,320]{1,0,2:T(4,128)(2,1)S(1)} %copy.142), channel_id=1, replica_groups=mesh['dp'=64,'seq'=4] {'seq'}, dimensions={2}, use_global_device_ids=true | all-gather | bytes 960000 | tf_op jit(solution)/shard_map/all_gather | solution.py:74
  35.3 2.8 copy.144
  49.2 2.4 fusion.38
  54.5 2.7 convolution_convert_fusion
  57.5 3.6 copy.143
  61.6 2.7 reshape.169
  65.3 2.7 convolution_convert_fusion.1
  69.7 3.5 reshape.191
  73.4 35.5 %all-reduce.6.cloned.1.call-done = bf16[300,1280]{1,0:T(8,128)(2,1)} async-done(((bf16[300,1280]{1,0:T(8,128)(2,1)}), bf16[300,1280]{1,0:T(8,128)(2,1)}) %all-reduce.6.cloned.1.call-update) | async-done | bytes 768016 | tf_op jit(solution)/shard_map/psum | solution.py:91
  108.9 2.9 convert_add_fusion
  111.8 3.0 reshape.167
  114.8 3.2 reduce_sum.84
  118.5 18.7 %reduce-scatter.4.cloned.1.call-done = bf16[320,150]{1,0:T(8,128)(2,1)} async-done(((bf16[1280,150]{1,0:T(8,128)(2,1)}), bf16[320,150]{1,0:T(8,128)(2,1)}) %reduce-scatter.4.cloned.1.call-update) | async-done | bytes 96016
  139.0 16.6 %all_gather.7 = bf16[3,50,1280]{1,0,2:T(4,128)(2,1)} all-gather(bf16[3,50,320]{1,0,2:T(4,128)(2,1)} %bitcast.58), channel_id=1, replica_groups=mesh['dp'=64,'seq'=4] {'seq'}, dimensions={2}, use_global_device_ids=true | all-gather | bytes 480000 | tf_op jit(solution)/shard_map/all_gather | solution.py:120
  155.5 2.6 copy.156
  165.3 2.4 convolution_convert_fusion.6
  171.8 2.4 fusion.9
  190.9 4.7 %convolution_bitcast_fusion = f32[3,1280,320]{1,2,0:T(8,128)} fusion(bf16[300,1280,1]{1,0,2:T(8,128)(2,1)S(1)} %copy-done.3, bf16[1,300,320]{2,1,0:T(8,128)(2,1)} %reshape.190, bf16[1,300,320]{2,1,0:T(8,128)(2,1)} %reshape.189, bf16[1,300,320]{2,1,0:T(8,128)(2,1)S(1)} %reshape.188), kind=kOutput, calls=%fused_computation.3 | convolution fusion | flops 737856000 | bytes 6259200 | tf_op jit(solution)/shard_map/rd,jre->jde/dot_general | solution.py:142
  195.7 9.1 %copy.172 = f32[3,1280,320]{2,0,1:T(4,128)} copy(f32[3,1280,320]{1,2,0:T(8,128)} %convolution_bitcast_fusion) | data formatting | bytes 9830400 | tf_op jit(solution)/shard_map/rd,jre->jde/transpose | solution.py:142
  206.8 2.5 fusion.7
  211.3 3.5 all-to-all-start
  216.0 4.4 %all-to-all-done = bf16[4,40,896]{2,1,0:T(8,128)(2,1)S(1)} async-done(((bf16[4,40,896]{2,1,0:T(8,128)(2,1)}), bf16[4,40,896]{2,1,0:T(8,128)(2,1)S(1)}, u32[]{:S(2)}, u32[]{:S(2)}) %all-to-all-start) | async-done | bytes 286752 | tf_op jit(solution)/shard_map/all_to_all | solution.py:110
  221.1 194.4 %all-reduce.8.cloned.1.call-done = (f32[3,1280,320]{2,0,1:T(4,128)}, f32[320,1280]{0,1:T(8,128)}) async-done(((f32[3,1280,320]{2,0,1:T(4,128)}, f32[320,1280]{0,1:T(8,128)}), (f32[3,1280,320]{2,0,1:T(4,128)}, f32[320,1280]{0,1:T(8,128)})) %all-reduce.8.cloned.1.call-update) | async-done | bytes 6553616
  (104 shorter events, 63.5 us)
Async XLA Ops:
  7.2 31.9 %copy-start = (bf16[3,1280,320]{1,2,0:T(8,128)(2,1)S(1)}, bf16[3,1280,320]{1,2,0:T(8,128)(2,1)}, u32[]{:S(2)}) copy-start(bf16[3,1280,320]{1,2,0:T(8,128)(2,1)} %param.12) | copy-start | bytes 7372804
  9.0 55.3 %all-to-all-start.1 = ((bf16[40,4,896]{2,0,1:T(8,128)(2,1)}), bf16[40,4,896]{2,0,1:T(8,128)(2,1)S(1)}, u32[]{:S(2)}, u32[]{:S(2)}) async-start(bf16[40,4,896]{2,0,1:T(8,128)(2,1)} %bitcast.54), calls=%async_computation.1 | async-start | bytes 573440 | tf_op jit(solution)/shard_map/all_to_all | solution.py:111
  13.9 95.0 %all-reduce.6.cloned.1.call-start = ((), (), s32[]{:S(2)}) async-start(), calls=%async_computation.3 | async-start | bytes 1556480 | tf_op jit(solution)/shard_map/psum | solution.py:91
  31.0 2.8 copy-start.1
  43.5 5.6 %copy-start.14 = (s32[3]{0:T(128)S(1)}, s32[3]{0:T(128)}, u32[]{:S(2)}) copy-start(s32[3]{0:T(128)} %param.10) | copy-start | bytes 40
  49.2 2.4 copy-start.16
  51.6 0.6 copy-start.9
  54.0 3.3 copy-start.11
  54.5 6.6 %copy-start.4 = (bf16[300,320]{0,1:T(8,128)(2,1)}, bf16[300,320]{0,1:T(8,128)(2,1)S(1)}, u32[]{:S(2)}) copy-start(bf16[300,320]{0,1:T(8,128)(2,1)S(1)} %reshape.166) | copy-start | bytes 576004
  57.2 79.9 %reduce-scatter.4.cloned.1.call-start = ((), (), s32[]{:S(2)}) async-start(), calls=%async_computation.4 | async-start | bytes 819200
  61.6 3.7 copy-start.12
  73.2 342.3 %all-reduce.8.cloned.1.call-start = ((), (), s32[]{:S(2)}) async-start(), calls=%async_computation.5 | async-start | bytes 19660800
  163.0 8.8 %copy-start.6 = (bf16[3,100,5,64]{1,3,2,0:T(8,128)(2,1)S(1)}, bf16[3,100,5,64]{1,3,2,0:T(8,128)(2,1)}, u32[]{:S(2)}) copy-start(bf16[3,100,5,64]{1,3,2,0:T(8,128)(2,1)} %copy.148) | copy-start | bytes 576004
  163.0 8.8 %copy-start.10 = (f32[3,5,100]{2,1,0:T(8,128)S(1)}, f32[3,5,100]{2,1,0:T(8,128)}, u32[]{:S(2)}) copy-start(f32[3,5,100]{2,1,0:T(8,128)} %copy-done.9) | copy-start | bytes 18004
  163.0 8.8 %copy-start.17 = (pred[3,100]{1,0:T(4,128)(4,1)S(1)}, pred[3,100]{1,0:T(4,128)(4,1)}, u32[]{:S(2)}) copy-start(pred[3,100]{1,0:T(4,128)(4,1)} %copy-done.16) | copy-start | bytes 904
  174.2 1.9 copy-start.8
  176.1 1.3 copy-start.7
  176.1 1.5 copy-start.5
  181.9 9.0 %copy-start.3 = (bf16[300,1280,1]{1,0,2:T(8,128)(2,1)S(1)}, bf16[300,1280,1]{1,0,2:T(8,128)(2,1)}, u32[]{:S(2)}) copy-start(bf16[300,1280,1]{1,0,2:T(8,128)(2,1)} %reshape.186) | copy-start | bytes 2304004
  204.7 1.2 copy-start.2
  204.7 2.1 copy-start.13
  206.8 7.9 %copy-start.15 = (u32[256]{0:T(256)S(1)}, u32[256]{0:T(256)}, u32[]{:S(2)}) copy-start(u32[256]{0:T(256)} %constant.54) | copy-start | bytes 3076
  211.3 9.1 %all-to-all-start = ((bf16[4,40,896]{2,1,0:T(8,128)(2,1)}), bf16[4,40,896]{2,1,0:T(8,128)(2,1)S(1)}, u32[]{:S(2)}, u32[]{:S(2)}) async-start(bf16[4,40,896]{2,1,0:T(8,128)(2,1)} %bitcast.4), calls=%async_computation | async-start | bytes 573440 | tf_op jit(solution)/shard_map/all_to_all | solution.py:110
Sparse Core Ops, SparseCore 0:
  57.4 51.5 all-reduce.5
  111.4 25.6 reduce-scatter.3
  204.9 210.6 all-reduce.7
where the time goes:
time: 428 us; the launch traced here: 425 us
  waiting for transfers between devices  253 us (59%)
  local copies, waits for them, and re-layouts  72.2 us (17%)
  blocking collectives  31.8 us (7%)
  matrix products  29.4 us (7%)
  between operations  15.3 us (4%)
  other arithmetic  14.8 us (3%)
  starting transfers between devices  8.56 us (2%)
    unnamed x5, waiting for transfers between devices  213 us
    psum x1, waiting for transfers between devices, shards(): lax.psum(head_terms.astype(jnp.bfloat16), 'seq').astype(jnp.float32)  35.5 us
    all_gather x1, blocking collectives, shards(): lax.all_gather(adapted_grad, 'seq', axis=2, tiled=True).astype(jnp.float32)  16.6 us
    all_gather x1, blocking collectives, shards(): full_audio = lax.all_gather(audio, 'seq', axis=2, tiled=True)  15.3 us
    unnamed x44, local copies, waits for them, and re-layouts  13.3 us
    another operation x6, local copies, waits for them, and re-layouts, shards(): jnp.stack([query_grad, key_grad, value_grad])  11.2 us
    transpose x1, local copies, waits for them, and re-layouts, shards(): jnp.einsum('rd,jre->jde', normed_half, stacked, preferred_element_type=jn...  9.06 us
  transfers between devices with their start and end apart: 5, of which 4 were waited for; matrix products, arithmetic and copies ran while one was open for 14% of the time, Pallas kernels for 0%

commit v1 on v0

v1 whole, which is shorter than its diff:
```python
import functools

import jax
import jax.numpy as jnp
from jax import lax
from jax.experimental import pallas as pl
from jax.experimental.pallas import tpu as pltpu
from jax.sharding import PartitionSpec as P

MESH = pl.DeviceIdType.MESH
F32 = jnp.float32
BF16 = jnp.bfloat16
EPSILON = 1e-05
SCALING = 0.125
PARTS = (
    (0, 0, 160, "ABa"),
    (1, 0, 160, "BAb"),
    (2, 0, 160, "aAB"),
    (3, 0, 160, "bBA"),
    (4, 0, 80, "ABa"),
    (4, 80, 80, "BAb"),
)


def dot(a, b):
    return jnp.dot(a, b, preferred_element_type=F32)


def dot_nt(a, b):
    return lax.dot_general(a, b, (((1,), (1,)), ((), ())), preferred_element_type=F32)


def dot_tn(a, b):
    return lax.dot_general(a, b, (((0,), (0,)), ((), ())), preferred_element_type=F32)


def fold(rows, width, extra):
    pieces = [rows[:, i : i + width] for i in range(0, rows.shape[1], width)]
    if extra:
        pieces.append(jnp.zeros((extra, width), F32))
    return jnp.concatenate(pieces, axis=0).astype(BF16)


def unfold(folded, count):
    wide = folded.astype(F32)
    return jnp.concatenate([wide[40 * i : 40 * i + 40] for i in range(count)], axis=1)


def normalize(rows):
    centred = rows - jnp.mean(rows, axis=-1, keepdims=True)
    inverse = lax.rsqrt(jnp.mean(centred * centred, axis=-1, keepdims=True) + EPSILON)
    return centred * inverse, inverse


def received_shape(part, step):
    _, _, rows, order = part
    before = order[:step]
    y_done = sum(letter in "AB" for letter in before)
    z_done = any(letter in "ab" for letter in before)
    if order[step] in "AB":
        return (2 if y_done == 0 else 1, 1 if z_done else 2, rows, 128)
    return ((4, 2, 1)[y_done], 1, rows, 128)


def kernel(whole, *refs):
    (counts, lengths, positions, audio, cotangent, w_qkv, w_out, w_proj) = refs[:8]
    embeds, grad_qkv, grad_out = refs[8:11]
    (
        wq, wo, wp, tmp, aud, cot_s, cot_r, gt_s, gt_r, t_s, t_r, ag_a, ad_a, e_s, e_r,
        nb, nt, pj, q2s, qr_s, k_s, v_s, prob, attp_s, agt, mgp, dqk, dvs, grad, core_r, total, final,
        z_s, z_r, f_s, f_r, w_sem, x_send, x_recv, c_send, c_recv, r_send, r_recv, z_send, z_recv,
    ) = refs[11 : 11 + 45]
    r_bufs = refs[11 + 45 :]

    dp = lax.axis_index("dp")
    x = lax.axis_index("seq")
    y = dp // 16
    z = (dp // 2) % 8
    c = dp % 2
    par = z % 2
    zp = z // 2

    def at(yy, zz, cc):
        return (yy * 16 + zz * 2 + cc, x)

    peers = [(dp, (x + k) % 4) for k in (1, 2, 3)]
    partner = {
        "A": at(y ^ 1, z, c),
        "B": at(y ^ 3, z, c),
        "a": at(y, z ^ 1, c),
        "b": at(y, (z + 7 + 2 * par) % 8, c),
    }
    core_peer = at(y, z, 1 - c)
    z_peers = [at(y, z ^ (2 * k), c) for k in (1, 2, 3)]

    weight_copies = []
    for s in range(4):
        weight_copies.append((w_qkv.at[:, pl.ds(320 * s, 256)], wq.at[:, pl.ds(256 * s, 256)]))
        weight_copies.append((w_qkv.at[:, pl.ds(320 * s + 256, 64)], wq.at[:, pl.ds(1024 + 64 * s, 64)]))
    weight_copies.append((w_out, wo))
    weight_copies.append((w_proj, wp))
    weight_copies = [
        pltpu.make_async_copy(src, dst, w_sem.at[i]) for i, (src, dst) in enumerate(weight_copies)
    ]
    for copy in weight_copies:
        copy.start()

    barrier = pltpu.get_barrier_semaphore()
    everyone = peers + ([core_peer] + list(partner.values()) + z_peers if whole else [])
    for device in everyone:
        pl.semaphore_signal(barrier, inc=1, device_id=device, device_id_type=MESH)

    lane = lax.broadcasted_iota(jnp.int32, (112, 128), 1)
    low = lane < 64
    tmp[...] = jnp.zeros_like(tmp)
    pj[...] = jnp.zeros_like(pj)
    mgp[...] = jnp.zeros_like(mgp)
    for b in range(3):
        tmp[b, 0:100, 0:320] = audio[b].astype(F32)
        packed = tmp[b, 0:64, 256:384] + pltpu.roll(tmp[b, 64:128, 256:384], 64, 1)
        own = jnp.concatenate([tmp[b, 0:112, 0:128], tmp[b, 0:112, 128:256], packed], axis=0)
        aud[x, b] = own.astype(BF16)
    cot_rows = cotangent[...].astype(F32)
    for t in range(4):
        cot_s[t] = fold(cot_rows[:, 896 * t : 896 * t + 896], 128, 8)
    cot_r[x] = cot_s[x]

    pl.semaphore_wait(barrier, len(everyone))

    started = []

    def to_peers(slot, source, target):
        copies = []
        for k in (1, 2, 3):
            there = (x + k) % 4
            copy = pltpu.make_async_remote_copy(
                src_ref=source(there),
                dst_ref=target(k),
                send_sem=x_send.at[slot, k - 1],
                recv_sem=x_recv.at[slot, k - 1],
                device_id=(dp, there),
                device_id_type=MESH,
            )
            copy.start()
            copies.append(copy)
        started.extend(copies)
        return copies

    def arrive(copies):
        for copy in copies:
            copy.wait_recv()

    audio_copies = []
    for b in range(3):
        block = aud.at[x, b]
        audio_copies.append(to_peers(b, lambda there: block, lambda k: block))
        if b == 1:
            cot_copies = to_peers(3, lambda there: cot_s.at[there], lambda k: cot_r.at[x])

    pos_pad = jnp.concatenate([positions[...].astype(F32), jnp.zeros((13, 50), F32)], axis=0).astype(BF16)
    frame_row = lax.broadcasted_iota(jnp.int32, (50, 112), 0)
    frame_col = lax.broadcasted_iota(jnp.int32, (50, 112), 1)
    spread = jnp.where(frame_row == frame_col // 2, 1.0, 0.0).astype(BF16)
    pos_lanes = dot(pos_pad, spread)
    frame_row_t = lax.broadcasted_iota(jnp.int32, (112, 50), 0)
    frame_col_t = lax.broadcasted_iota(jnp.int32, (112, 50), 1)
    spread_t = jnp.where(frame_row_t // 2 == frame_col_t, 1.0, 0.0).astype(BF16)
    pos_sub = dot_nt(spread_t, pos_pad)
    lives = [jnp.where(b < counts[0], lengths[b], 0) for b in range(3)]

    def place(b, first, count):
        row = lax.broadcasted_iota(jnp.int32, (count, 112), 0) + first
        frame = lax.broadcasted_iota(jnp.int32, (count, 112), 1)
        hit = (row.astype(F32) == pos_lanes[b : b + 1, :]) & (frame < lives[b])
        return jnp.where(hit, 1.0, 0.0).astype(BF16)

    def unplace(b):
        frame = lax.broadcasted_iota(jnp.int32, (112, 160), 0)
        row = lax.broadcasted_iota(jnp.int32, (112, 160), 1)
        hit = (row.astype(F32) == pos_sub[:, b : b + 1]) & (frame < lives[b])
        return jnp.where(hit, 1.0, 0.0).astype(BF16)

    def split_heads(tile):
        return jnp.concatenate([jnp.where(low, tile, 0.0), jnp.where(low, 0.0, tile)], axis=0).astype(BF16)

    for copy in weight_copies[:8]:
        copy.wait()

    attp = [jnp.zeros((160, 128), F32) for _ in range(3)]
    pooled_audio = jnp.zeros((40, 1280), F32)

    def forward(b, attp, pooled_audio):
        arrive(audio_copies[b])
        tiles = []
        for s in range(4):
            tiles.append(aud[s, b, 0:112].astype(F32))
            tiles.append(aud[s, b, 112:224].astype(F32))
        for s in (0, 2):
            left = aud[s, b, 224:288].astype(F32)
            right = aud[s + 1, b, 224:288].astype(F32)
            left_turned = pltpu.roll(left, 64, 1)
            right_turned = pltpu.roll(right, 64, 1)
            top = jnp.where(low[0:64], left, right_turned)
            bottom = jnp.where(low[0:64], left_turned, right)
            tiles.append(jnp.concatenate([top, bottom[0:48]], axis=0))
        frames = jnp.concatenate(tiles, axis=1)
        pooled_audio = pooled_audio + dot(place(b, 40 * x, 40), frames.astype(BF16))
        normed = normalize(frames)[0].astype(BF16)
        nb[112 * b : 112 * b + 112, :] = normed
        for j in range(3):
            pj[j, :, 0:320] = dot(normed, wq[j])
        k_s[b] = pj[1].astype(BF16)
        v_s[b] = pj[2].astype(BF16)
        key_limit = jnp.maximum(lives[b], 1)
        placed = place(b, 0, 160)
        for g in range(3):
            cols = slice(128 * g, 128 * g + 128)
            q_tile = pj[0, :, cols]
            if g < 2:
                queries = split_heads(q_tile)
                q2s[b, g] = queries
            else:
                queries = q_tile.astype(BF16)
                qr_s[b] = queries
            rows = queries.shape[0]
            scores = dot_nt(queries, k_s[b, :, cols]) * SCALING
            key = lax.broadcasted_iota(jnp.int32, (rows, 112), 1)
            scores = jnp.where(key < key_limit, scores, -1e30)
            powered = jnp.exp(scores - jnp.max(scores, axis=-1, keepdims=True))
            weights = powered * (1.0 / jnp.sum(powered, axis=-1, keepdims=True))
            prob[b, g, 0:rows] = weights
            mixed = dot(weights.astype(BF16), v_s[b, :, cols])
            if g < 2:
                mixed = jnp.where(low, mixed[0:112], mixed[112:224])
            attp[g] = attp[g] + dot(placed, mixed.astype(BF16))
        return attp, pooled_audio

    attp, pooled_audio = forward(0, attp, pooled_audio)
    attp, pooled_audio = forward(1, attp, pooled_audio)

    weight_copies[9].wait()
    arrive(cot_copies)
    row_grads = jnp.concatenate([unfold(cot_r[s], 7) for s in range(4)], axis=0).astype(BF16)
    adapter_terms = dot_nt(row_grads, wp[...])
    for t in range(4):
        gt_s[t] = fold(adapter_terms[40 * t : 40 * t + 40], 640, 0)
    gt_copies = to_peers(4, lambda there: gt_s.at[there], lambda k: gt_r.at[k - 1])

    attp, pooled_audio = forward(2, attp, pooled_audio)
    for g in range(3):
        attp_s[g] = attp[g].astype(BF16)
    weight_copies[8].wait()
    head_terms = (
        dot(attp_s[0], wo[0:128]) + dot(attp_s[1], wo[128:256]) + dot(attp_s[2][:, 0:64], wo[256:320])
    )
    for t in range(4):
        t_s[t] = fold(head_terms[40 * t : 40 * t + 40], 640, 0)
    t_copies = to_peers(5, lambda there: t_s.at[there], lambda k: t_r.at[k - 1])

    nt[...] = nb[...].T
    pooled_audio = jnp.concatenate(
        [
            piece
            for s in range(4)
            for piece in (
                pooled_audio[:, 256 * s : 256 * s + 256],
                pooled_audio[:, 1024 + 64 * s : 1088 + 64 * s],
            )
        ],
        axis=1,
    )

    arrive(gt_copies)
    adapted_grad = gt_s[x].astype(F32)
    for k in range(3):
        adapted_grad = adapted_grad + gt_r[k].astype(F32)
    adapted_grad = unfold(adapted_grad.astype(BF16), 2)

    arrive(t_copies)
    attention = t_s[x].astype(F32)
    for k in range(3):
        attention = attention + t_r[k].astype(F32)
    attention = jnp.concatenate([attention[0:40], attention[40:80]], axis=1)
    normed_rows, inverse = normalize((pooled_audio + attention) * 0.5)
    pooled_grad = inverse * (
        adapted_grad
        - jnp.mean(adapted_grad, axis=-1, keepdims=True)
        - normed_rows * jnp.mean(adapted_grad * normed_rows, axis=-1, keepdims=True)
    )
    ag_a[x] = fold(pooled_grad * 0.5, 640, 0)
    ag_copies = to_peers(6, lambda there: ag_a.at[x], lambda k: ag_a.at[x])
    ad_a[x] = fold(normed_rows, 640, 0)
    ad_copies = to_peers(7, lambda there: ad_a.at[x], lambda k: ad_a.at[x])

    arrive(ag_copies)
    attention_grad = jnp.concatenate([unfold(ag_a[s], 2) for s in range(4)], axis=0).astype(BF16)
    agt[...] = attention_grad.T
    mgp[:, 0:320] = dot_nt(attention_grad, wo[...]).astype(BF16)

    for b in range(3):
        rows = slice(112 * b, 112 * b + 112)
        mixed_grad = dot(unplace(b), mgp[...])
        for g in range(3):
            cols = slice(128 * g, 128 * g + 128)
            tile = mixed_grad[:, cols]
            if g < 2:
                grads, queries, count = split_heads(tile), q2s[b, g], 224
            else:
                grads, queries, count = tile.astype(BF16), qr_s[b], 112
            weights = prob[b, g, 0:count]
            prob_grad = dot_nt(grads, v_s[b, :, cols])
            inner = jnp.sum(weights * prob_grad, axis=-1, keepdims=True)
            score_half = (weights * (prob_grad - inner)).astype(BF16)
            query_grad = dot(score_half, k_s[b, :, cols])
            if g < 2:
                query_grad = jnp.where(low, query_grad[0:112], query_grad[112:224])
            query_grad = query_grad * SCALING
            key_grad = dot_tn(score_half, queries) * SCALING
            value_grad = dot_tn(weights.astype(BF16), grads)
            dvs[rows, cols] = value_grad.astype(BF16)
            if g < 2:
                dqk[rows, cols] = query_grad.astype(BF16)
                dqk[rows, 256 + 128 * g : 384 + 128 * g] = key_grad.astype(BF16)
            else:
                dqk[rows, 512:640] = (query_grad + pltpu.roll(key_grad, 64, 1)).astype(BF16)

    attp_turned = pltpu.roll(attp_s[2].astype(F32), 64, 1).astype(BF16)
    core_copies = []
    for yy in range(4):
        features = jnp.concatenate(
            [nt[256 * yy : 256 * yy + 256, :], nt[1024 + 64 * yy : 1088 + 64 * yy, :]], axis=0
        )
        backs = agt[320 * yy : 320 * yy + 320, :]
        first = dot(features, dqk[...])
        value_part = dot(features, dvs[...])
        out_part = [dot(backs, attp_s[0]), dot(backs, attp_s[1]), dot(backs, attp_turned)]
        halves = (
            [first[:, 128 * t : 128 * t + 128] for t in range(5)],
            [value_part[:, 0:128], value_part[:, 128:256], out_part[0], out_part[1], value_part[:, 256:384] + out_part[2]],
        )
        for half in range(2):
            for t in range(5):
                for side in range(2):
                    grad[half, yy, t, side] = jnp.concatenate(
                        [halves[half][t][40 * i : 40 * i + 40] for i in range(side, 8, 2)], axis=0
                    ).astype(BF16)
        if whole:
            copy = pltpu.make_async_remote_copy(
                src_ref=grad.at[1 - c, yy],
                dst_ref=core_r.at[yy],
                send_sem=c_send.at[yy],
                recv_sem=c_recv.at[yy],
                device_id=core_peer,
                device_id_type=MESH,
            )
            copy.start()
            core_copies.append(copy)
    started.extend(core_copies)

    def start_embeds():
        arrive(ad_copies)
        adapted = jnp.concatenate([unfold(ad_a[s], 2) for s in range(4)], axis=0).astype(BF16)
        adapter_rows = dot(adapted, wp[...])
        for t in range(4):
            e_s[t] = fold(adapter_rows[40 * t : 40 * t + 40], 128, 8)
        e_r[x] = e_s[x]
        return to_peers(8, lambda there: e_s.at[there], lambda k: e_r.at[x])

    def finish_embeds(copies):
        arrive(copies)
        for s in range(4):
            embeds[:, 896 * s : 896 * s + 896] = unfold(e_r[s], 7).astype(BF16)

    if not whole:
        finish_embeds(start_embeds())
        grad_qkv[...] = grad[...].astype(F32)
        grad_out[...] = jnp.zeros_like(grad_out)
        for copy in started:
            copy.wait_send()
        return

    for yy in range(4):
        core_copies[yy].wait_recv()
        total[yy] = (grad[c, yy].astype(F32) + core_r[yy].astype(F32)).astype(BF16)

    def blocks(order, step):
        y_before = [letter for letter in order[:step] if letter in "AB"]
        z_done = any(letter in "ab" for letter in order[:step])
        letter = order[step]
        if letter in "AB":
            near = y ^ (1 if letter == "A" else 3)
            other = y ^ (3 if letter == "A" else 1)
            sides = (par, par) if z_done else (None, None)
            if y_before:
                return [near], [y], sides
            return [near, y ^ 2], [y, other], sides
        held = [0, 1, 2, 3]
        if len(y_before) == 1:
            held = [y, y ^ (3 if y_before[0] == "A" else 1)]
        elif len(y_before) == 2:
            held = [y]
        return held, held, (1 - par, par)

    def begin(p, step):
        tile, row, count, order = PARTS[p]
        send, _, (side, _) = blocks(order, step)
        landing = r_bufs[3 * p + step]
        copies = []
        for i, block in enumerate(send):
            pick = pl.ds(0, 2) if side is None else pl.ds(side, 1)
            copy = pltpu.make_async_remote_copy(
                src_ref=total.at[block, tile, pick, pl.ds(row, count)],
                dst_ref=landing.at[i],
                send_sem=r_send.at[p, step, i],
                recv_sem=r_recv.at[p, step, i],
                device_id=partner[order[step]],
                device_id_type=MESH,
            )
            copy.start()
            copies.append(copy)
        started.extend(copies)
        return copies

    def end(p, step, copies):
        tile, row, count, order = PARTS[p]
        _, keep, (_, side) = blocks(order, step)
        landing = r_bufs[3 * p + step]
        rows = pl.ds(row, count)
        arrive(copies)
        for i, block in enumerate(keep):
            if step == 2:
                final[tile, rows] = total[block, tile, par, rows].astype(F32) + landing[i, 0].astype(F32)
            elif side is None:
                for k in range(2):
                    kept = total[block, tile, k, rows].astype(F32) + landing[i, k].astype(F32)
                    total[block, tile, k, rows] = kept.astype(BF16)
            else:
                kept = total[block, tile, side, rows].astype(F32) + landing[i, 0].astype(F32)
                total[block, tile, side, rows] = kept.astype(BF16)

    flying = [begin(p, 0) for p in range(len(PARTS))]
    embed_copies = start_embeds()
    for step in (1, 2):
        for p in range(len(PARTS)):
            end(p, step - 1, flying[p])
            flying[p] = begin(p, step)
    for p in range(len(PARTS)):
        end(p, 2, flying[p])

    for j in range(4):
        z_s[j] = jnp.concatenate(
            [final[t, 40 * j : 40 * j + 40] for t in range(5)] + [jnp.zeros((8, 128), F32)], axis=0
        ).astype(BF16)
    z_copies = []
    for k in (1, 2, 3):
        copy = pltpu.make_async_remote_copy(
            src_ref=z_s.at[zp ^ k],
            dst_ref=z_r.at[k - 1],
            send_sem=z_send.at[k - 1],
            recv_sem=z_recv.at[k - 1],
            device_id=z_peers[k - 1],
            device_id_type=MESH,
        )
        copy.start()
        z_copies.append(copy)
    started.extend(z_copies)
    finish_embeds(embed_copies)
    arrive(z_copies)
    mine = z_s[zp].astype(F32)
    for k in range(3):
        mine = mine + z_r[k].astype(F32)
    first_core = c == 0
    own_tiles = []
    f_s[...] = jnp.zeros_like(f_s)
    for t in range(5):
        rows = mine[40 * t : 40 * t + 40]
        early, late = rows[0:20], rows[20:40]
        own_tiles.append(jnp.where(first_core, early, late))
        f_s[t, 0:20] = jnp.where(first_core, late, early).astype(BF16)
    copy = pltpu.make_async_remote_copy(
        src_ref=f_s,
        dst_ref=f_r,
        send_sem=c_send.at[4],
        recv_sem=c_recv.at[4],
        device_id=core_peer,
        device_id_type=MESH,
    )
    copy.start()
    started.append(copy)
    copy.wait_recv()
    for t in range(5):
        got = f_r[t, 0:20].astype(F32)
        left = jnp.where(first_core, own_tiles[t], got)
        right = jnp.where(first_core, got, own_tiles[t])
        if t < 2:
            cols = slice(128 * t, 128 * t + 128)
            grad_qkv[0, :, cols] = left
            grad_qkv[2, :, cols] = right
        elif t < 4:
            cols = slice(128 * t - 256, 128 * t - 128)
            grad_qkv[1, :, cols] = left
            grad_out[:, cols] = right
        else:
            grad_qkv[0, :, 256:320] = left[:, 0:64]
            grad_qkv[1, :, 256:320] = left[:, 64:128]
            grad_qkv[2, :, 256:320] = right[:, 0:64]
            grad_out[:, 256:320] = right[:, 64:128]
    for copy in started:
        copy.wait_send()


def call(whole, counts, lengths, positions, audio, cotangent, w_qkv, w_out, w_proj):
    vmem, dma = pltpu.VMEM, pltpu.SemaphoreType.DMA
    scratch = [
        vmem((3, 1280, 320), BF16),
        vmem((320, 1280), BF16),
        vmem((1280, 896), BF16),
        vmem((3, 128, 384), F32),
        vmem((4, 3, 288, 128), BF16),
        vmem((4, 288, 128), BF16),
        vmem((4, 288, 128), BF16),
        vmem((4, 80, 640), BF16),
        vmem((3, 80, 640), BF16),
        vmem((4, 80, 640), BF16),
        vmem((3, 80, 640), BF16),
        vmem((4, 80, 640), BF16),
        vmem((4, 80, 640), BF16),
        vmem((4, 288, 128), BF16),
        vmem((4, 288, 128), BF16),
        vmem((336, 1280), BF16),
        vmem((1280, 336), BF16),
        vmem((3, 112, 384), F32),
        vmem((3, 2, 224, 128), BF16),
        vmem((3, 112, 128), BF16),
        vmem((3, 112, 384), BF16),
        vmem((3, 112, 384), BF16),
        vmem((3, 3, 224, 112), F32),
        vmem((3, 160, 128), BF16),
        vmem((1280, 160), BF16),
        vmem((160, 384), BF16),
        vmem((336, 640), BF16),
        vmem((336, 384), BF16),
        vmem((2, 4, 5, 2, 160, 128), BF16),
        vmem((4, 5, 2, 160, 128), BF16),
        vmem((4, 5, 2, 160, 128), BF16),
        vmem((5, 160, 128), F32),
        vmem((4, 208, 128), BF16),
        vmem((3, 208, 128), BF16),
        vmem((5, 32, 128), BF16),
        vmem((5, 32, 128), BF16),
        dma((10,)),
        dma((9, 3)),
        dma((9, 3)),
        dma((5,)),
        dma((5,)),
        dma((6, 3, 4)),
        dma((6, 3, 4)),
        dma((3,)),
        dma((3,)),
    ]
    assert len(scratch) == 45
    scratch += [vmem(received_shape(part, step), BF16) for part in PARTS for step in range(3)]
    in_vmem = pl.BlockSpec(memory_space=pltpu.VMEM)
    in_smem = pl.BlockSpec(memory_space=pltpu.SMEM)
    anywhere = pl.BlockSpec(memory_space=pl.ANY)
    gq = (3, 20, 320) if whole else (2, 4, 5, 2, 160, 128)
    return pl.pallas_call(
        functools.partial(kernel, whole),
        out_shape=(
            jax.ShapeDtypeStruct((40, 3584), BF16),
            jax.ShapeDtypeStruct(gq, F32),
            jax.ShapeDtypeStruct((20, 320), F32),
        ),
        in_specs=[in_smem, in_smem, in_vmem, in_vmem, in_vmem, anywhere, anywhere, anywhere],
        out_specs=(in_vmem, in_vmem, in_vmem),
        scratch_shapes=scratch,
        compiler_params=pltpu.CompilerParams(
            collective_id=0, has_side_effects=True, vmem_limit_bytes=56 * 2**20
        ),
        name="sublayer",
    )(counts, lengths, positions, audio, cotangent, w_qkv, w_out, w_proj)


def shards(audio, counts, lengths, positions, w_qkv, w_out, w_proj, cotangent):
    embeds, grad_qkv, grad_out = call(
        True, counts, lengths, positions, audio, cotangent, w_qkv, w_out, w_proj
    )
    return embeds, grad_qkv, grad_out.T


def solution(mesh):
    in_specs = (
        P("dp", None, "seq"),
        P("dp"),
        P("dp"),
        P("dp", None),
        P(None, None, "seq"),
        P("seq", None),
        P(None, "seq"),
        P(("dp", "seq"), None),
    )
    out_specs = (P(("dp", "seq"), None), P(None, "dp", "seq"), P("seq", "dp"))
    return jax.shard_map(shards, mesh=mesh, in_specs=in_specs, out_specs=out_specs, check_vma=False)
```

time: 428 us -> 90.5 us (0.21)
  waiting for transfers between devices: 253 us -> 0 us
  Pallas kernels: 0 us -> 79 us
  local copies, waits for them, and re-layouts: 72.2 us -> 9.88 us
  blocking collectives: 31.8 us -> 0 us
  matrix products: 29.4 us -> 0 us
  other arithmetic: 14.8 us -> 0 us
  between operations: 15.3 us -> 1.29 us
  starting transfers between devices: 8.56 us -> 0 us
    unnamed x5 -> x0, waiting for transfers between devices: 213 us -> none
    pallas_call x0 -> x1, Pallas kernels: none -> 79 us  [call(): pl.pallas_call(functools.partial(kernel, whole), out_shape=(jax.ShapeDtyp...]
    psum x1 -> x0, waiting for transfers between devices: 35.5 us -> none  [shards(): lax.psum(head_terms.astype(jnp.bfloat16), 'seq').astype(jnp.float32)]
    all_gather x2 -> x0, blocking collectives: 31.8 us -> none  [the longest x1 16.6 us: shards(): lax.all_gather(adapted_grad, 'seq', axis=2, tiled=True).astype(jnp.float32)]
    dot_general x12 -> x0, matrix products: 26.9 us -> none  [the longest x1 4.75 us: shards(): jnp.einsum('rd,jre->jde', normed_half, stacked, preferred_element_type=jn...]
    convert_element_type x6 -> x0, local copies, waits for them, and re-layouts: 11.7 us -> none  [the longest x2 6.29 us: shards(): full_audio.reshape(row_total, model_width).astype(jnp.float32) + attention]
    another operation x6 -> x0, local copies, waits for them, and re-layouts: 11.2 us -> none  [shards(): jnp.stack([query_grad, key_grad, value_grad])]
    transpose x1 -> x0, local copies, waits for them, and re-layouts: 9.06 us -> none  [shards(): jnp.einsum('rd,jre->jde', normed_half, stacked, preferred_element_type=jn...]
  transfers between devices with their start and end apart: 5 -> 0, of which waited for: 4 -> 0; matrix products, arithmetic and copies ran while one was open for 14% -> 0% of each run, Pallas kernels for 0% -> 0%
where the time goes in v1:
time: 90.5 us; the launch traced here: 90.1 us
  Pallas kernels  79 us (87%)
  local copies, waits for them, and re-layouts  9.88 us (11%)
  between operations  1.29 us (1%)
    pallas_call x1, Pallas kernels, call(): pl.pallas_call(functools.partial(kernel, whole), out_shape=(jax.ShapeDtyp...  79 us
    unnamed x4, local copies, waits for them, and re-layouts  9.88 us

profile of v1, /device:TPU:1, one launch (start us, length us, event | category | flops | bytes accessed | tf_op | source)
XLA Modules:
  0.0 90.1 jit_solution(821534880460970425)
XLA Ops:
  1.3 5.3 %copy.11.refs_5_ = bf16[3,1280,320]{2,1,0:T(8,128)(2,1)} copy(bf16[3,1280,320]{1,2,0:T(8,128)(2,1)} %param.12) | data formatting | bytes 4915200 | tf_op args[4]
  6.5 79.0 %sublayer.1 = (bf16[40,3584]{1,0:T(8,128)(2,1)}, f32[3,20,320]{2,1,0:T(8,128)}, f32[20,320]{1,0:T(8,128)}) custom-call(s32[1]{0:T(128)S(6)} %copy.15.refs_0_, s32[3]{0:T(128)} %refs_1_.1, s32[3,50]{1,0:T(4,128)} %refs_2_.1, bf16[3,100,320]{2,1,0:T(8,128)(2,1)} %refs_3_.1, bf16[40,3584]{1,0:T(8,128)(2,1)} %refs_4_.1, bf16[3,1280,320]{2,1,0:T(8,128)(2,1)} %copy.11.refs_5_, ...), custom_call_target="tpu_custom_call" | custom-call | tf_op jit(solution)/shard_map/sublayer/pallas_call | solution.py:567
  85.5 1.7 %copy.16 = bf16[40,3584]{1,0:T(8,128)(2,1)} copy(bf16[40,3584]{1,0:T(8,128)(2,1)} %get-tuple-element.12) | data formatting | bytes 573440
  87.2 1.5 %copy.17 = f32[3,20,320]{2,1,0:T(8,128)} copy(f32[3,20,320]{2,1,0:T(8,128)} %get-tuple-element.13) | data formatting | bytes 153600
  88.7 1.4 %copy.18 = f32[320,20]{0,1:T(8,128)} copy(f32[320,20]{0,1:T(8,128)} %bitcast.1) | data formatting | bytes 51200

commit v2 on v1

--- a/solution.py
+++ b/solution.py
@@ -66,11 +66,11 @@
     (counts, lengths, positions, audio, cotangent, w_qkv, w_out, w_proj) = refs[:8]
     embeds, grad_qkv, grad_out = refs[8:11]
     (
-        wq, wo, wp, tmp, aud, cot_s, cot_r, gt_s, gt_r, t_s, t_r, ag_a, ad_a, e_s, e_r,
+        wq, wo, wp, tmp, aud, cot_s, cot_r, gt_s, gt_r, t_s, t_r, ag_a, ad_a, e_s, e_r, cot_v, aud_v, emb,
         nb, nt, pj, q2s, qr_s, k_s, v_s, prob, attp_s, agt, mgp, dqk, dvs, grad, core_r, total, final,
         z_s, z_r, f_s, f_r, w_sem, x_send, x_recv, c_send, c_recv, r_send, r_recv, z_send, z_recv,
-    ) = refs[11 : 11 + 45]
-    r_bufs = refs[11 + 45 :]
+    ) = refs[11 : 11 + 48]
+    r_bufs = refs[11 + 48 :]
 
     dp = lax.axis_index("dp")
     x = lax.axis_index("seq")
@@ -93,16 +93,15 @@
     core_peer = at(y, z, 1 - c)
     z_peers = [at(y, z ^ (2 * k), c) for k in (1, 2, 3)]
 
-    weight_copies = []
-    for s in range(4):
-        weight_copies.append((w_qkv.at[:, pl.ds(320 * s, 256)], wq.at[:, pl.ds(256 * s, 256)]))
-        weight_copies.append((w_qkv.at[:, pl.ds(320 * s + 256, 64)], wq.at[:, pl.ds(1024 + 64 * s, 64)]))
-    weight_copies.append((w_out, wo))
-    weight_copies.append((w_proj, wp))
+    input_copies = [
+        pltpu.make_async_copy(src, dst, w_sem.at[3 + i])
+        for i, (src, dst) in enumerate(((cotangent, cot_v), (audio, aud_v)))
+    ]
     weight_copies = [
-        pltpu.make_async_copy(src, dst, w_sem.at[i]) for i, (src, dst) in enumerate(weight_copies)
+        pltpu.make_async_copy(src, dst, w_sem.at[i])
+        for i, (src, dst) in enumerate(((w_qkv, wq), (w_out, wo), (w_proj, wp)))
     ]
-    for copy in weight_copies:
+    for copy in input_copies:
         copy.start()
 
     barrier = pltpu.get_barrier_semaphore()
@@ -110,25 +109,44 @@
     for device in everyone:
         pl.semaphore_signal(barrier, inc=1, device_id=device, device_id_type=MESH)
 
+    for i in (2, 0, 1):
+        weight_copies[i].start()
+
     lane = lax.broadcasted_iota(jnp.int32, (112, 128), 1)
     low = lane < 64
+    low_half = low[0:64]
     tmp[...] = jnp.zeros_like(tmp)
     pj[...] = jnp.zeros_like(pj)
     mgp[...] = jnp.zeros_like(mgp)
-    for b in range(3):
-        tmp[b, 0:100, 0:320] = audio[b].astype(F32)
-        packed = tmp[b, 0:64, 256:384] + pltpu.roll(tmp[b, 64:128, 256:384], 64, 1)
-        own = jnp.concatenate([tmp[b, 0:112, 0:128], tmp[b, 0:112, 128:256], packed], axis=0)
-        aud[x, b] = own.astype(BF16)
-    cot_rows = cotangent[...].astype(F32)
+    input_copies[0].wait()
+    cot_rows = cot_v[...].astype(F32)
     for t in range(4):
         cot_s[t] = fold(cot_rows[:, 896 * t : 896 * t + 896], 128, 8)
     cot_r[x] = cot_s[x]
 
+    def pack_audio(b):
+        tmp[b, 0:100, 0:320] = aud_v[b].astype(F32)
+        first, second, third = (tmp[b, :, 128 * i : 128 * i + 128] for i in range(3))
+        second_turned = pltpu.roll(second, 64, 1)
+        packed = third[0:64] + pltpu.roll(third[64:128], 64, 1)
+        packed_odd = jnp.where(low_half, first[0:64], pltpu.roll(first[64:128], 64, 1))
+        even = jnp.concatenate([first[0:112], second[0:112], packed], axis=0)
+        odd = jnp.concatenate(
+            [
+                jnp.where(low, pltpu.roll(first, 64, 1)[0:112], second_turned[0:112]),
+                jnp.where(low, second_turned[0:112], pltpu.roll(third, 64, 1)[0:112]),
+                packed_odd,
+            ],
+            axis=0,
+        )
+        aud[x, b] = jnp.where(x % 2 == 0, even, odd).astype(BF16)
+
+    input_copies[1].wait()
+    pack_audio(0)
+
     pl.semaphore_wait(barrier, len(everyone))
 
     started = []
-
     def to_peers(slot, source, target):
         copies = []
         for k in (1, 2, 3):
@@ -151,11 +169,12 @@
             copy.wait_recv()
 
     audio_copies = []
+    cot_copies = to_peers(3, lambda there: cot_s.at[there], lambda k: cot_r.at[x])
     for b in range(3):
+        if b > 0:
+            pack_audio(b)
         block = aud.at[x, b]
         audio_copies.append(to_peers(b, lambda there: block, lambda k: block))
-        if b == 1:
-            cot_copies = to_peers(3, lambda there: cot_s.at[there], lambda k: cot_r.at[x])
 
     pos_pad = jnp.concatenate([positions[...].astype(F32), jnp.zeros((13, 50), F32)], axis=0).astype(BF16)
     frame_row = lax.broadcasted_iota(jnp.int32, (50, 112), 0)
@@ -183,8 +202,7 @@
     def split_heads(tile):
         return jnp.concatenate([jnp.where(low, tile, 0.0), jnp.where(low, 0.0, tile)], axis=0).astype(BF16)
 
-    for copy in weight_copies[:8]:
-        copy.wait()
+    weight_copies[0].wait()
 
     attp = [jnp.zeros((160, 128), F32) for _ in range(3)]
     pooled_audio = jnp.zeros((40, 1280), F32)
@@ -192,23 +210,22 @@
     def forward(b, attp, pooled_audio):
         arrive(audio_copies[b])
         tiles = []
-        for s in range(4):
-            tiles.append(aud[s, b, 0:112].astype(F32))
-            tiles.append(aud[s, b, 112:224].astype(F32))
         for s in (0, 2):
             left = aud[s, b, 224:288].astype(F32)
             right = aud[s + 1, b, 224:288].astype(F32)
-            left_turned = pltpu.roll(left, 64, 1)
-            right_turned = pltpu.roll(right, 64, 1)
-            top = jnp.where(low[0:64], left, right_turned)
-            bottom = jnp.where(low[0:64], left_turned, right)
+            top = jnp.where(low_half, left, pltpu.roll(right, 64, 1))
+            bottom = jnp.where(low_half, pltpu.roll(left, 64, 1), right)
+            tiles.append(aud[s, b, 0:112].astype(F32))
+            tiles.append(aud[s, b, 112:224].astype(F32))
             tiles.append(jnp.concatenate([top, bottom[0:48]], axis=0))
+            tiles.append(aud[s + 1, b, 0:112].astype(F32))
+            tiles.append(aud[s + 1, b, 112:224].astype(F32))
         frames = jnp.concatenate(tiles, axis=1)
         pooled_audio = pooled_audio + dot(place(b, 40 * x, 40), frames.astype(BF16))
         normed = normalize(frames)[0].astype(BF16)
         nb[112 * b : 112 * b + 112, :] = normed
         for j in range(3):
-            pj[j, :, 0:320] = dot(normed, wq[j])
+            pj[j, :, 0:320] = dot_nt(normed, wq[j])
         k_s[b] = pj[1].astype(BF16)
         v_s[b] = pj[2].astype(BF16)
         key_limit = jnp.maximum(lives[b], 1)
@@ -236,20 +253,20 @@
         return attp, pooled_audio
 
     attp, pooled_audio = forward(0, attp, pooled_audio)
-    attp, pooled_audio = forward(1, attp, pooled_audio)
-
-    weight_copies[9].wait()
+
+    weight_copies[2].wait()
     arrive(cot_copies)
     row_grads = jnp.concatenate([unfold(cot_r[s], 7) for s in range(4)], axis=0).astype(BF16)
     adapter_terms = dot_nt(row_grads, wp[...])
     for t in range(4):
         gt_s[t] = fold(adapter_terms[40 * t : 40 * t + 40], 640, 0)
+    attp, pooled_audio = forward(1, attp, pooled_audio)
     gt_copies = to_peers(4, lambda there: gt_s.at[there], lambda k: gt_r.at[k - 1])
 
     attp, pooled_audio = forward(2, attp, pooled_audio)
     for g in range(3):
         attp_s[g] = attp[g].astype(BF16)
-    weight_copies[8].wait()
+    weight_copies[1].wait()
     head_terms = (
         dot(attp_s[0], wo[0:128]) + dot(attp_s[1], wo[128:256]) + dot(attp_s[2][:, 0:64], wo[256:320])
     )
@@ -258,17 +275,6 @@
     t_copies = to_peers(5, lambda there: t_s.at[there], lambda k: t_r.at[k - 1])
 
     nt[...] = nb[...].T
-    pooled_audio = jnp.concatenate(
-        [
-            piece
-            for s in range(4)
-            for piece in (
-                pooled_audio[:, 256 * s : 256 * s + 256],
-                pooled_audio[:, 1024 + 64 * s : 1088 + 64 * s],
-            )
-        ],
-        axis=1,
-    )
 
     arrive(gt_copies)
     adapted_grad = gt_s[x].astype(F32)
@@ -327,9 +333,7 @@
     attp_turned = pltpu.roll(attp_s[2].astype(F32), 64, 1).astype(BF16)
     core_copies = []
     for yy in range(4):
-        features = jnp.concatenate(
-            [nt[256 * yy : 256 * yy + 256, :], nt[1024 + 64 * yy : 1088 + 64 * yy, :]], axis=0
-        )
+        features = nt[320 * yy : 320 * yy + 320, :]
         backs = agt[320 * yy : 320 * yy + 320, :]
         first = dot(features, dqk[...])
         value_part = dot(features, dvs[...])
@@ -369,10 +373,13 @@
     def finish_embeds(copies):
         arrive(copies)
         for s in range(4):
-            embeds[:, 896 * s : 896 * s + 896] = unfold(e_r[s], 7).astype(BF16)
+            emb[:, 896 * s : 896 * s + 896] = unfold(e_r[s], 7).astype(BF16)
+        copy = pltpu.make_async_copy(emb, embeds, w_sem.at[5])
+        copy.start()
+        return copy
 
     if not whole:
-        finish_embeds(start_embeds())
+        finish_embeds(start_embeds()).wait()
         grad_qkv[...] = grad[...].astype(F32)
         grad_out[...] = jnp.zeros_like(grad_out)
         for copy in started:
@@ -440,10 +447,12 @@
 
     flying = [begin(p, 0) for p in range(len(PARTS))]
     embed_copies = start_embeds()
-    for step in (1, 2):
-        for p in range(len(PARTS)):
-            end(p, step - 1, flying[p])
-            flying[p] = begin(p, step)
+    for p in range(len(PARTS)):
+        end(p, 0, flying[p])
+        flying[p] = begin(p, 1)
+    for p in range(len(PARTS)):
+        end(p, 1, flying[p])
+        flying[p] = begin(p, 2)
     for p in range(len(PARTS)):
         end(p, 2, flying[p])
 
@@ -464,7 +473,7 @@
         copy.start()
         z_copies.append(copy)
     started.extend(z_copies)
-    finish_embeds(embed_copies)
+    embeds_copy = finish_embeds(embed_copies)
     arrive(z_copies)
     mine = z_s[zp].astype(F32)
     for k in range(3):
@@ -487,7 +496,7 @@
     )
     copy.start()
     started.append(copy)
-    copy.wait_recv()
+    arrive([copy])
     for t in range(5):
         got = f_r[t, 0:20].astype(F32)
         left = jnp.where(first_core, own_tiles[t], got)
@@ -505,6 +514,7 @@
             grad_qkv[1, :, 256:320] = left[:, 64:128]
             grad_qkv[2, :, 256:320] = right[:, 0:64]
             grad_out[:, 256:320] = right[:, 64:128]
+    embeds_copy.wait()
     for copy in started:
         copy.wait_send()
 
@@ -512,7 +522,7 @@
 def call(whole, counts, lengths, positions, audio, cotangent, w_qkv, w_out, w_proj):
     vmem, dma = pltpu.VMEM, pltpu.SemaphoreType.DMA
     scratch = [
-        vmem((3, 1280, 320), BF16),
+        vmem((3, 320, 1280), BF16),
         vmem((320, 1280), BF16),
         vmem((1280, 896), BF16),
         vmem((3, 128, 384), F32),
@@ -527,6 +537,9 @@
         vmem((4, 80, 640), BF16),
         vmem((4, 288, 128), BF16),
         vmem((4, 288, 128), BF16),
+        vmem((40, 3584), BF16),
+        vmem((3, 100, 320), BF16),
+        vmem((40, 3584), BF16),
         vmem((336, 1280), BF16),
         vmem((1280, 336), BF16),
         vmem((3, 112, 384), F32),
@@ -548,7 +561,7 @@
         vmem((3, 208, 128), BF16),
         vmem((5, 32, 128), BF16),
         vmem((5, 32, 128), BF16),
-        dma((10,)),
+        dma((6,)),
         dma((9, 3)),
         dma((9, 3)),
         dma((5,)),
@@ -558,7 +571,7 @@
         dma((3,)),
         dma((3,)),
     ]
-    assert len(scratch) == 45
+    assert len(scratch) == 48
     scratch += [vmem(received_shape(part, step), BF16) for part in PARTS for step in range(3)]
     in_vmem = pl.BlockSpec(memory_space=pltpu.VMEM)
     in_smem = pl.BlockSpec(memory_space=pltpu.SMEM)
@@ -571,20 +584,42 @@
             jax.ShapeDtypeStruct(gq, F32),
             jax.ShapeDtypeStruct((20, 320), F32),
         ),
-        in_specs=[in_smem, in_smem, in_vmem, in_vmem, in_vmem, anywhere, anywhere, anywhere],
-        out_specs=(in_vmem, in_vmem, in_vmem),
+        in_specs=[in_smem, in_smem, in_vmem] + [anywhere] * 5,
+        out_specs=(anywhere, in_vmem, in_vmem),
         scratch_shapes=scratch,
         compiler_params=pltpu.CompilerParams(
-            collective_id=0, has_side_effects=True, vmem_limit_bytes=56 * 2**20
+            collective_id=0, has_side_effects=True, vmem_limit_bytes=60 * 2**20
         ),
         name="sublayer",
     )(counts, lengths, positions, audio, cotangent, w_qkv, w_out, w_proj)
 
 
+def write_out(*refs):
+    sources, targets, sems = refs[:3], refs[3:6], refs[6]
+    copies = [pltpu.make_async_copy(sources[i], targets[i], sems.at[i]) for i in range(3)]
+    for copy in copies:
+        copy.start()
+    for copy in copies:
+        copy.wait()
+
+
+def results(*parts):
+    anywhere = pl.BlockSpec(memory_space=pl.ANY)
+    return pl.pallas_call(
+        write_out,
+        out_shape=tuple(jax.ShapeDtypeStruct(part.shape, part.dtype) for part in parts),
+        in_specs=[anywhere] * 3,
+        out_specs=(anywhere,) * 3,
+        scratch_shapes=[pltpu.SemaphoreType.DMA((3,))],
+        name="results",
+    )(*parts)
+
+
 def shards(audio, counts, lengths, positions, w_qkv, w_out, w_proj, cotangent):
     embeds, grad_qkv, grad_out = call(
-        True, counts, lengths, positions, audio, cotangent, w_qkv, w_out, w_proj
+        True, counts, lengths, positions, audio, cotangent, jnp.swapaxes(w_qkv, 1, 2), w_out, w_proj
     )
+    embeds, grad_qkv, grad_out = results(embeds, grad_qkv, grad_out)
     return embeds, grad_qkv, grad_out.T
 
 

time: 90.5 us -> 95.6 us (1.056)
  Pallas kernels: 79 us -> 94.2 us
  local copies, waits for them, and re-layouts: 9.88 us -> 0 us
    pallas_call x0 -> x1, Pallas kernels: none -> 14.3 us  [results(): pl.pallas_call(write_out, out_shape=tuple((jax.ShapeDtypeStruct(part.shap...]
    unnamed x4 -> x0, local copies, waits for them, and re-layouts: 9.88 us -> none
    pallas_call x1, Pallas kernels: 79 us -> 80 us  [call(): pl.pallas_call(functools.partial(kernel, whole), out_shape=(jax.ShapeDtyp...]
where the time goes in v2:
time: 95.6 us; the launch traced here: 95.5 us
  Pallas kernels  94.2 us (99%)
  between operations  1.29 us (1%)
    pallas_call x1, Pallas kernels, call(): pl.pallas_call(functools.partial(kernel, whole), out_shape=(jax.ShapeDtyp...  80 us
    pallas_call x1, Pallas kernels, results(): pl.pallas_call(write_out, out_shape=tuple((jax.ShapeDtypeStruct(part.shap...  14.3 us

profile of v2, /device:TPU:1, one launch (start us, length us, event | category | flops | bytes accessed | tf_op | source)
XLA Modules:
  0.0 95.5 jit_solution(7559503732035893250)
XLA Ops:
  1.3 80.0 %sublayer.1 = (bf16[40,3584]{1,0:T(8,128)(2,1)}, f32[3,20,320]{2,1,0:T(8,128)}, f32[20,320]{1,0:T(8,128)}) custom-call(s32[1]{0:T(128)S(6)} %copy.11.refs_0_, s32[3]{0:T(128)} %refs_1_.1, s32[3,50]{1,0:T(4,128)} %refs_2_.1, bf16[3,100,320]{2,1,0:T(8,128)(2,1)} %refs_3_.1, bf16[40,3584]{1,0:T(8,128)(2,1)} %refs_4_.1, bf16[3,320,1280]{2,1,0:T(8,128)(2,1)} %bitcast.2, ...), custom_call_target="tpu_custom_call" | custom-call | tf_op jit(solution)/shard_map/sublayer/pallas_call | solution.py:580
  81.2 14.3 %results.1 = (bf16[40,3584]{1,0:T(8,128)(2,1)}, f32[3,20,320]{2,1,0:T(8,128)}, f32[20,320]{1,0:T(8,128)}) custom-call(bf16[40,3584]{1,0:T(8,128)(2,1)} %get-tuple-element.9.refs_0_, f32[3,20,320]{2,1,0:T(8,128)} %get-tuple-element.10.refs_1_, f32[20,320]{1,0:T(8,128)} %get-tuple-element.11.refs_2_), custom_call_target="tpu_custom_call" | custom-call | tf_op jit(solution)/shard_map/results/pallas_call | solution.py:608

commit v3 on v2

--- a/solution.py
+++ b/solution.py
@@ -1,5 +1,3 @@
-import functools
-
 import jax
 import jax.numpy as jnp
 from jax import lax
@@ -22,6 +20,10 @@
 )
 
 
+TURNS = (2, 3, 0, 1, 4, 5)
+Z_GROUPS = (((0, 1), 0, 80), ((2, 3), 80, 80), ((4,), 160, 48))
+
+
 def dot(a, b):
     return jnp.dot(a, b, preferred_element_type=F32)
 
@@ -62,15 +64,15 @@
     return ((4, 2, 1)[y_done], 1, rows, 128)
 
 
-def kernel(whole, *refs):
+def kernel(*refs):
     (counts, lengths, positions, audio, cotangent, w_qkv, w_out, w_proj) = refs[:8]
     embeds, grad_qkv, grad_out = refs[8:11]
     (
         wq, wo, wp, tmp, aud, cot_s, cot_r, gt_s, gt_r, t_s, t_r, ag_a, ad_a, e_s, e_r, cot_v, aud_v, emb,
-        nb, nt, pj, q2s, qr_s, k_s, v_s, prob, attp_s, agt, mgp, dqk, dvs, grad, core_r, total, final,
+        nb, nt, pj, q2s, qr_s, k_s, v_s, prob, attp_s, agt, mgp, local, other, total, final,
         z_s, z_r, f_s, f_r, w_sem, x_send, x_recv, c_send, c_recv, r_send, r_recv, z_send, z_recv,
-    ) = refs[11 : 11 + 48]
-    r_bufs = refs[11 + 48 :]
+    ) = refs[11 : 11 + 46]
+    r_bufs = refs[11 + 46 :]
 
     dp = lax.axis_index("dp")
     x = lax.axis_index("seq")
@@ -105,7 +107,7 @@
         copy.start()
 
     barrier = pltpu.get_barrier_semaphore()
-    everyone = peers + ([core_peer] + list(partner.values()) + z_peers if whole else [])
+    everyone = peers + [core_peer] + list(partner.values()) + z_peers
     for device in everyone:
         pl.semaphore_signal(barrier, inc=1, device_id=device, device_id_type=MESH)
 
@@ -118,6 +120,7 @@
     tmp[...] = jnp.zeros_like(tmp)
     pj[...] = jnp.zeros_like(pj)
     mgp[...] = jnp.zeros_like(mgp)
+    local[1, :, 384:640] = jnp.zeros((336, 256), BF16)
     input_copies[0].wait()
     cot_rows = cot_v[...].astype(F32)
     for t in range(4):
@@ -163,6 +166,19 @@
             copies.append(copy)
         started.extend(copies)
         return copies
+
+    def to_core(slot, source, target):
+        copy = pltpu.make_async_remote_copy(
+            src_ref=source,
+            dst_ref=target,
+            send_sem=c_send.at[slot],
+            recv_sem=c_recv.at[slot],
+            device_id=core_peer,
+            device_id_type=MESH,
+        )
+        copy.start()
+        started.append(copy)
+        return copy
 
     def arrive(copies):
         for copy in copies:
@@ -264,17 +280,20 @@
     gt_copies = to_peers(4, lambda there: gt_s.at[there], lambda k: gt_r.at[k - 1])
 
     attp, pooled_audio = forward(2, attp, pooled_audio)
-    for g in range(3):
-        attp_s[g] = attp[g].astype(BF16)
+    attp = [part.astype(BF16) for part in attp]
+    for g in range(2):
+        attp_s[c, :, 128 * g : 128 * g + 128] = attp[g]
+    attp_s[c, :, 256:384] = pltpu.roll(attp[2].astype(F32), 64, 1).astype(BF16)
     weight_copies[1].wait()
     head_terms = (
-        dot(attp_s[0], wo[0:128]) + dot(attp_s[1], wo[128:256]) + dot(attp_s[2][:, 0:64], wo[256:320])
+        dot(attp[0], wo[0:128]) + dot(attp[1], wo[128:256]) + dot(attp[2][:, 0:64], wo[256:320])
     )
     for t in range(4):
         t_s[t] = fold(head_terms[40 * t : 40 * t + 40], 640, 0)
     t_copies = to_peers(5, lambda there: t_s.at[there], lambda k: t_r.at[k - 1])
 
-    nt[...] = nb[...].T
+    nt[c] = nb[...].T
+    core_copies = [to_core(0, nt.at[c], nt.at[c]), to_core(1, attp_s.at[c], attp_s.at[c])]
 
     arrive(gt_copies)
     adapted_grad = gt_s[x].astype(F32)
@@ -296,11 +315,11 @@
     ag_a[x] = fold(pooled_grad * 0.5, 640, 0)
     ag_copies = to_peers(6, lambda there: ag_a.at[x], lambda k: ag_a.at[x])
     ad_a[x] = fold(normed_rows, 640, 0)
+    arrive(ag_copies)
     ad_copies = to_peers(7, lambda there: ad_a.at[x], lambda k: ad_a.at[x])
-
-    arrive(ag_copies)
     attention_grad = jnp.concatenate([unfold(ag_a[s], 2) for s in range(4)], axis=0).astype(BF16)
-    agt[...] = attention_grad.T
+    agt[c] = attention_grad.T
+    core_copies.append(to_core(2, agt.at[c], agt.at[c]))
     mgp[:, 0:320] = dot_nt(attention_grad, wo[...]).astype(BF16)
 
     for b in range(3):
@@ -323,43 +342,14 @@
             query_grad = query_grad * SCALING
             key_grad = dot_tn(score_half, queries) * SCALING
             value_grad = dot_tn(weights.astype(BF16), grads)
-            dvs[rows, cols] = value_grad.astype(BF16)
+            local[1, rows, cols] = value_grad.astype(BF16)
             if g < 2:
-                dqk[rows, cols] = query_grad.astype(BF16)
-                dqk[rows, 256 + 128 * g : 384 + 128 * g] = key_grad.astype(BF16)
+                local[0, rows, cols] = query_grad.astype(BF16)
+                local[0, rows, 256 + 128 * g : 384 + 128 * g] = key_grad.astype(BF16)
             else:
-                dqk[rows, 512:640] = (query_grad + pltpu.roll(key_grad, 64, 1)).astype(BF16)
-
-    attp_turned = pltpu.roll(attp_s[2].astype(F32), 64, 1).astype(BF16)
-    core_copies = []
-    for yy in range(4):
-        features = nt[320 * yy : 320 * yy + 320, :]
-        backs = agt[320 * yy : 320 * yy + 320, :]
-        first = dot(features, dqk[...])
-        value_part = dot(features, dvs[...])
-        out_part = [dot(backs, attp_s[0]), dot(backs, attp_s[1]), dot(backs, attp_turned)]
-        halves = (
-            [first[:, 128 * t : 128 * t + 128] for t in range(5)],
-            [value_part[:, 0:128], value_part[:, 128:256], out_part[0], out_part[1], value_part[:, 256:384] + out_part[2]],
-        )
-        for half in range(2):
-            for t in range(5):
-                for side in range(2):
-                    grad[half, yy, t, side] = jnp.concatenate(
-                        [halves[half][t][40 * i : 40 * i + 40] for i in range(side, 8, 2)], axis=0
-                    ).astype(BF16)
-        if whole:
-            copy = pltpu.make_async_remote_copy(
-                src_ref=grad.at[1 - c, yy],
-                dst_ref=core_r.at[yy],
-                send_sem=c_send.at[yy],
-                recv_sem=c_recv.at[yy],
-                device_id=core_peer,
-                device_id_type=MESH,
-            )
-            copy.start()
-            core_copies.append(copy)
-    started.extend(core_copies)
+                local[0, rows, 512:640] = (query_grad + pltpu.roll(key_grad, 64, 1)).astype(BF16)
+        block = pl.ds(112 * b, 112)
+        core_copies.append(to_core(3 + b, local.at[1 - c, block], other.at[block]))
 
     def start_embeds():
         arrive(ad_copies)
@@ -378,42 +368,32 @@
         copy.start()
         return copy
 
-    if not whole:
-        finish_embeds(start_embeds()).wait()
-        grad_qkv[...] = grad[...].astype(F32)
-        grad_out[...] = jnp.zeros_like(grad_out)
-        for copy in started:
-            copy.wait_send()
-        return
-
-    for yy in range(4):
-        core_copies[yy].wait_recv()
-        total[yy] = (grad[c, yy].astype(F32) + core_r[yy].astype(F32)).astype(BF16)
-
     def blocks(order, step):
         y_before = [letter for letter in order[:step] if letter in "AB"]
         z_done = any(letter in "ab" for letter in order[:step])
         letter = order[step]
         if letter in "AB":
             near = y ^ (1 if letter == "A" else 3)
-            other = y ^ (3 if letter == "A" else 1)
+            beyond = y ^ (3 if letter == "A" else 1)
             sides = (par, par) if z_done else (None, None)
             if y_before:
                 return [near], [y], sides
-            return [near, y ^ 2], [y, other], sides
-        held = [0, 1, 2, 3]
+            return [y ^ 2, near], [beyond, y], sides
+        held = [y ^ 2, y ^ 1, y ^ 3, y]
         if len(y_before) == 1:
-            held = [y, y ^ (3 if y_before[0] == "A" else 1)]
+            held = [y ^ (3 if y_before[0] == "A" else 1), y]
         elif len(y_before) == 2:
             held = [y]
         return held, held, (1 - par, par)
 
-    def begin(p, step):
+    def begin(p, step, only=None):
         tile, row, count, order = PARTS[p]
         send, _, (side, _) = blocks(order, step)
         landing = r_bufs[3 * p + step]
         copies = []
         for i, block in enumerate(send):
+            if only is not None and i != only:
+                continue
             pick = pl.ds(0, 2) if side is None else pl.ds(side, 1)
             copy = pltpu.make_async_remote_copy(
                 src_ref=total.at[block, tile, pick, pl.ds(row, count)],
@@ -445,34 +425,72 @@
                 kept = total[block, tile, side, rows].astype(F32) + landing[i, 0].astype(F32)
                 total[block, tile, side, rows] = kept.astype(BF16)
 
-    flying = [begin(p, 0) for p in range(len(PARTS))]
+    arrive(core_copies)
+    flying = {(p, 0): [] for p in range(len(PARTS))}
+    turns = (y ^ 2, y ^ 1, y ^ 3, y)
+    for turn, yy in enumerate(turns):
+        rows = pl.ds(pl.multiple_of(320 * yy, 64), 320)
+
+        def store(tile, values):
+            for side in range(2):
+                total[yy, tile, side] = jnp.concatenate(
+                    [values[40 * i : 40 * i + 40] for i in range(side, 8, 2)], axis=0
+                ).astype(BF16)
+
+        @pl.when(c == 0)
+        def _():
+            part = dot(nt[0, rows], local[0]) + dot(nt[1, rows], other[...])
+            for t in range(5):
+                store(t, part[:, 128 * t : 128 * t + 128])
+
+        @pl.when(c == 1)
+        def _():
+            value_part = dot(nt[1, rows], local[1, :, 0:384]) + dot(nt[0, rows], other[:, 0:384])
+            out_part = dot(agt[0, rows], attp_s[0]) + dot(agt[1, rows], attp_s[1])
+            store(0, value_part[:, 0:128])
+            store(1, value_part[:, 128:256])
+            store(2, out_part[:, 0:128])
+            store(3, out_part[:, 128:256])
+            store(4, value_part[:, 256:384] + out_part[:, 256:384])
+
+        for p, part in enumerate(PARTS):
+            slots = {"A": (0, 1, None, None), "B": (0, None, 1, None)}.get(part[3][0], (0, 1, 2, 3))
+            if slots[turn] is not None:
+                flying[p, 0] += begin(p, 0, slots[turn])
     embed_copies = start_embeds()
-    for p in range(len(PARTS)):
-        end(p, 0, flying[p])
-        flying[p] = begin(p, 1)
-    for p in range(len(PARTS)):
-        end(p, 1, flying[p])
-        flying[p] = begin(p, 2)
-    for p in range(len(PARTS)):
-        end(p, 2, flying[p])
-
-    for j in range(4):
-        z_s[j] = jnp.concatenate(
-            [final[t, 40 * j : 40 * j + 40] for t in range(5)] + [jnp.zeros((8, 128), F32)], axis=0
-        ).astype(BF16)
     z_copies = []
-    for k in (1, 2, 3):
-        copy = pltpu.make_async_remote_copy(
-            src_ref=z_s.at[zp ^ k],
-            dst_ref=z_r.at[k - 1],
-            send_sem=z_send.at[k - 1],
-            recv_sem=z_recv.at[k - 1],
-            device_id=z_peers[k - 1],
-            device_id_type=MESH,
-        )
-        copy.start()
-        z_copies.append(copy)
-    started.extend(z_copies)
+
+    def last_exchange(group):
+        tiles, first, count = Z_GROUPS[group]
+        fill = count - 40 * len(tiles)
+        for j in range(4):
+            pieces = [final[t, 40 * j : 40 * j + 40] for t in tiles]
+            if fill:
+                pieces.append(jnp.zeros((fill, 128), F32))
+            z_s[j, first : first + count] = jnp.concatenate(pieces, axis=0).astype(BF16)
+        for k in (1, 2, 3):
+            copy = pltpu.make_async_remote_copy(
+                src_ref=z_s.at[zp ^ k, pl.ds(first, count)],
+                dst_ref=z_r.at[k - 1, pl.ds(first, count)],
+                send_sem=z_send.at[group, k - 1],
+                recv_sem=z_recv.at[group, k - 1],
+                device_id=z_peers[k - 1],
+                device_id_type=MESH,
+            )
+            copy.start()
+            z_copies.append(copy)
+            started.append(copy)
+
+    for p in TURNS:
+        end(p, 0, flying[p, 0])
+        flying[p, 1] = begin(p, 1)
+    for p in TURNS:
+        end(p, 1, flying[p, 1])
+        flying[p, 2] = begin(p, 2)
+    for group, members in ((1, (2, 3)), (0, (0, 1)), (2, (4, 5))):
+        for p in members:
+            end(p, 2, flying[p, 2])
+        last_exchange(group)
     embeds_copy = finish_embeds(embed_copies)
     arrive(z_copies)
     mine = z_s[zp].astype(F32)
@@ -486,17 +504,7 @@
         early, late = rows[0:20], rows[20:40]
         own_tiles.append(jnp.where(first_core, early, late))
         f_s[t, 0:20] = jnp.where(first_core, late, early).astype(BF16)
-    copy = pltpu.make_async_remote_copy(
-        src_ref=f_s,
-        dst_ref=f_r,
-        send_sem=c_send.at[4],
-        recv_sem=c_recv.at[4],
-        device_id=core_peer,
-        device_id_type=MESH,
-    )
-    copy.start()
-    started.append(copy)
-    arrive([copy])
+    arrive([to_core(6, f_s, f_r)])
     for t in range(5):
         got = f_r[t, 0:20].astype(F32)
         left = jnp.where(first_core, own_tiles[t], got)
@@ -519,7 +527,7 @@
         copy.wait_send()
 
 
-def call(whole, counts, lengths, positions, audio, cotangent, w_qkv, w_out, w_proj):
+def call(counts, lengths, positions, audio, cotangent, w_qkv, w_out, w_proj):
     vmem, dma = pltpu.VMEM, pltpu.SemaphoreType.DMA
     scratch = [
         vmem((3, 320, 1280), BF16),
@@ -541,20 +549,18 @@
         vmem((3, 100, 320), BF16),
         vmem((40, 3584), BF16),
         vmem((336, 1280), BF16),
-        vmem((1280, 336), BF16),
+        vmem((2, 1280, 336), BF16),
         vmem((3, 112, 384), F32),
         vmem((3, 2, 224, 128), BF16),
         vmem((3, 112, 128), BF16),
         vmem((3, 112, 384), BF16),
         vmem((3, 112, 384), BF16),
         vmem((3, 3, 224, 112), F32),
-        vmem((3, 160, 128), BF16),
-        vmem((1280, 160), BF16),
+        vmem((2, 160, 384), BF16),
+        vmem((2, 1280, 160), BF16),
         vmem((160, 384), BF16),
+        vmem((2, 336, 640), BF16),
         vmem((336, 640), BF16),
-        vmem((336, 384), BF16),
-        vmem((2, 4, 5, 2, 160, 128), BF16),
-        vmem((4, 5, 2, 160, 128), BF16),
         vmem((4, 5, 2, 160, 128), BF16),
         vmem((5, 160, 128), F32),
         vmem((4, 208, 128), BF16),
@@ -564,24 +570,23 @@
         dma((6,)),
         dma((9, 3)),
         dma((9, 3)),
-        dma((5,)),
-        dma((5,)),
+        dma((7,)),
+        dma((7,)),
         dma((6, 3, 4)),
         dma((6, 3, 4)),
-        dma((3,)),
-        dma((3,)),
+        dma((3, 3)),
+        dma((3, 3)),
     ]
-    assert len(scratch) == 48
+    assert len(scratch) == 46
     scratch += [vmem(received_shape(part, step), BF16) for part in PARTS for step in range(3)]
     in_vmem = pl.BlockSpec(memory_space=pltpu.VMEM)
     in_smem = pl.BlockSpec(memory_space=pltpu.SMEM)
     anywhere = pl.BlockSpec(memory_space=pl.ANY)
-    gq = (3, 20, 320) if whole else (2, 4, 5, 2, 160, 128)
     return pl.pallas_call(
-        functools.partial(kernel, whole),
+        kernel,
         out_shape=(
             jax.ShapeDtypeStruct((40, 3584), BF16),
-            jax.ShapeDtypeStruct(gq, F32),
+            jax.ShapeDtypeStruct((3, 20, 320), F32),
             jax.ShapeDtypeStruct((20, 320), F32),
         ),
         in_specs=[in_smem, in_smem, in_vmem] + [anywhere] * 5,
@@ -595,29 +600,24 @@
 
 
 def write_out(*refs):
-    sources, targets, sems = refs[:3], refs[3:6], refs[6]
-    copies = [pltpu.make_async_copy(sources[i], targets[i], sems.at[i]) for i in range(3)]
-    for copy in copies:
-        copy.start()
-    for copy in copies:
-        copy.wait()
+    for source, target in zip(refs[:3], refs[3:]):
+        target[...] = source[...]
 
 
 def results(*parts):
-    anywhere = pl.BlockSpec(memory_space=pl.ANY)
+    in_vmem = pl.BlockSpec(memory_space=pltpu.VMEM)
     return pl.pallas_call(
         write_out,
         out_shape=tuple(jax.ShapeDtypeStruct(part.shape, part.dtype) for part in parts),
-        in_specs=[anywhere] * 3,
-        out_specs=(anywhere,) * 3,
-        scratch_shapes=[pltpu.SemaphoreType.DMA((3,))],
+        in_specs=[in_vmem] * 3,
+        out_specs=(in_vmem,) * 3,
         name="results",
     )(*parts)
 
 
 def shards(audio, counts, lengths, positions, w_qkv, w_out, w_proj, cotangent):
     embeds, grad_qkv, grad_out = call(
-        True, counts, lengths, positions, audio, cotangent, jnp.swapaxes(w_qkv, 1, 2), w_out, w_proj
+        counts, lengths, positions, audio, cotangent, jnp.swapaxes(w_qkv, 1, 2), w_out, w_proj
     )
     embeds, grad_qkv, grad_out = results(embeds, grad_qkv, grad_out)
     return embeds, grad_qkv, grad_out.T

time: 95.6 us -> 79 us (0.83)
  Pallas kernels: 94.2 us -> 77.5 us
    pallas_call x1, Pallas kernels: 14.3 us -> 1.78 us  [results(): pl.pallas_call(write_out, out_shape=tuple((jax.ShapeDtypeStruct(part.shap...]
    pallas_call x1, Pallas kernels: 80 us -> 75.8 us  [call(): pl.pallas_call(kernel, out_shape=(jax.ShapeDtypeStruct((40, 3584), BF16),...]
where the time goes in v3:
time: 79 us; the launch traced here: 78.8 us
  Pallas kernels  77.5 us (98%)
  between operations  1.29 us (2%)
    pallas_call x1, Pallas kernels, call(): pl.pallas_call(kernel, out_shape=(jax.ShapeDtypeStruct((40, 3584), BF16),...  75.8 us
    pallas_call x1, Pallas kernels, results(): pl.pallas_call(write_out, out_shape=tuple((jax.ShapeDtypeStruct(part.shap...  1.78 us

profile of v3, /device:TPU:1, one launch (start us, length us, event | category | flops | bytes accessed | tf_op | source)
XLA Modules:
  0.0 78.8 jit_solution(11984521077562081461)
XLA Ops:
  1.3 75.8 %sublayer.1 = (bf16[40,3584]{1,0:T(8,128)(2,1)}, f32[3,20,320]{2,1,0:T(8,128)}, f32[20,320]{1,0:T(8,128)}) custom-call(s32[1]{0:T(128)S(6)} %copy.11.refs_0_, s32[3]{0:T(128)} %refs_1_.1, s32[3,50]{1,0:T(4,128)} %refs_2_.1, bf16[3,100,320]{2,1,0:T(8,128)(2,1)} %refs_3_.1, bf16[40,3584]{1,0:T(8,128)(2,1)} %refs_4_.1, bf16[3,320,1280]{2,1,0:T(8,128)(2,1)} %bitcast.2, ...), custom_call_target="tpu_custom_call" | custom-call | tf_op jit(solution)/shard_map/sublayer/pallas_call | solution.py:585
  77.0 1.8 %results.1 = (bf16[40,3584]{1,0:T(8,128)(2,1)}, f32[3,20,320]{2,1,0:T(8,128)}, f32[20,320]{1,0:T(8,128)}) custom-call(bf16[40,3584]{1,0:T(8,128)(2,1)} %get-tuple-element.9.refs_0_, f32[3,20,320]{2,1,0:T(8,128)} %get-tuple-element.10.refs_1_, f32[20,320]{1,0:T(8,128)} %get-tuple-element.11.refs_2_), custom_call_target="tpu_custom_call" | custom-call | tf_op jit(solution)/shard_map/results/pallas_call | solution.py:609

commit v4 on v3

--- a/solution.py
+++ b/solution.py
@@ -10,17 +10,12 @@
 BF16 = jnp.bfloat16
 EPSILON = 1e-05
 SCALING = 0.125
-PARTS = (
-    (0, 0, 160, "ABa"),
-    (1, 0, 160, "BAb"),
-    (2, 0, 160, "aAB"),
-    (3, 0, 160, "bBA"),
-    (4, 0, 80, "ABa"),
-    (4, 80, 80, "BAb"),
+PARTS = tuple(
+    (tile, row, 80, order)
+    for row, orders in ((0, ("ABa", "BAb", "aAB", "bBA", "ABa")), (80, ("ABa", "BAb", "aAB", "bBA", "BAb")))
+    for tile, order in enumerate(orders)
 )
-
-
-TURNS = (2, 3, 0, 1, 4, 5)
+TURNS = (2, 3, 0, 1, 4, 7, 8, 5, 6, 9)
 Z_GROUPS = (((0, 1), 0, 80), ((2, 3), 80, 80), ((4,), 160, 48))
 
 
@@ -69,10 +64,10 @@
     embeds, grad_qkv, grad_out = refs[8:11]
     (
         wq, wo, wp, tmp, aud, cot_s, cot_r, gt_s, gt_r, t_s, t_r, ag_a, ad_a, e_s, e_r, cot_v, aud_v, emb,
-        nb, nt, pj, q2s, qr_s, k_s, v_s, prob, attp_s, agt, mgp, local, other, total, final,
+        nb, nt, pj, q2s, qr_s, k_s, v_s, prob, attp_s, agt, mgp, local, other, total, final, prob_t, up_s,
         z_s, z_r, f_s, f_r, w_sem, x_send, x_recv, c_send, c_recv, r_send, r_recv, z_send, z_recv,
-    ) = refs[11 : 11 + 46]
-    r_bufs = refs[11 + 46 :]
+    ) = refs[11 : 11 + 48]
+    r_bufs = refs[11 + 48 :]
 
     dp = lax.axis_index("dp")
     x = lax.axis_index("seq")
@@ -262,6 +257,11 @@
             powered = jnp.exp(scores - jnp.max(scores, axis=-1, keepdims=True))
             weights = powered * (1.0 / jnp.sum(powered, axis=-1, keepdims=True))
             prob[b, g, 0:rows] = weights
+            scores_t = dot_nt(k_s[b, :, cols], queries) * SCALING
+            key_t = lax.broadcasted_iota(jnp.int32, (112, rows), 0)
+            scores_t = jnp.where(key_t < key_limit, scores_t, -1e30)
+            powered_t = jnp.exp(scores_t - jnp.max(scores_t, axis=0, keepdims=True))
+            prob_t[b, g, :, 0:rows] = powered_t * (1.0 / jnp.sum(powered_t, axis=0, keepdims=True))
             mixed = dot(weights.astype(BF16), v_s[b, :, cols])
             if g < 2:
                 mixed = jnp.where(low, mixed[0:112], mixed[112:224])
@@ -293,6 +293,8 @@
     t_copies = to_peers(5, lambda there: t_s.at[there], lambda k: t_r.at[k - 1])
 
     nt[c] = nb[...].T
+    for b in range(3):
+        up_s[b] = unplace(b)
     core_copies = [to_core(0, nt.at[c], nt.at[c]), to_core(1, attp_s.at[c], attp_s.at[c])]
 
     arrive(gt_copies)
@@ -316,40 +318,47 @@
     ag_copies = to_peers(6, lambda there: ag_a.at[x], lambda k: ag_a.at[x])
     ad_a[x] = fold(normed_rows, 640, 0)
     arrive(ag_copies)
-    ad_copies = to_peers(7, lambda there: ad_a.at[x], lambda k: ad_a.at[x])
     attention_grad = jnp.concatenate([unfold(ag_a[s], 2) for s in range(4)], axis=0).astype(BF16)
-    agt[c] = attention_grad.T
-    core_copies.append(to_core(2, agt.at[c], agt.at[c]))
     mgp[:, 0:320] = dot_nt(attention_grad, wo[...]).astype(BF16)
-
+    pairs = [(b, g) for b in range(3) for g in range(3)]
+    grads, prob_grads, prob_grads_t, halves, halves_t = {}, {}, {}, {}, {}
+    for b in range(3):
+        mixed_grad = dot(up_s[b], mgp[...])
+        for g in range(3):
+            tile = mixed_grad[:, 128 * g : 128 * g + 128]
+            grads[b, g] = split_heads(tile) if g < 2 else tile.astype(BF16)
+    for b, g in pairs:
+        cols = slice(128 * g, 128 * g + 128)
+        prob_grads[b, g] = dot_nt(grads[b, g], v_s[b, :, cols])
+        prob_grads_t[b, g] = dot_nt(v_s[b, :, cols], grads[b, g])
+    for b, g in pairs:
+        count = 224 if g < 2 else 112
+        weights, weights_t = prob[b, g, 0:count], prob_t[b, g, :, 0:count]
+        inner = jnp.sum(weights * prob_grads[b, g], axis=-1, keepdims=True)
+        inner_t = jnp.sum(weights_t * prob_grads_t[b, g], axis=0, keepdims=True)
+        halves[b, g] = (weights * (prob_grads[b, g] - inner)).astype(BF16)
+        halves_t[b, g] = (weights_t * (prob_grads_t[b, g] - inner_t)).astype(BF16)
     for b in range(3):
         rows = slice(112 * b, 112 * b + 112)
-        mixed_grad = dot(unplace(b), mgp[...])
         for g in range(3):
             cols = slice(128 * g, 128 * g + 128)
-            tile = mixed_grad[:, cols]
-            if g < 2:
-                grads, queries, count = split_heads(tile), q2s[b, g], 224
-            else:
-                grads, queries, count = tile.astype(BF16), qr_s[b], 112
-            weights = prob[b, g, 0:count]
-            prob_grad = dot_nt(grads, v_s[b, :, cols])
-            inner = jnp.sum(weights * prob_grad, axis=-1, keepdims=True)
-            score_half = (weights * (prob_grad - inner)).astype(BF16)
-            query_grad = dot(score_half, k_s[b, :, cols])
+            count = 224 if g < 2 else 112
+            query_grad = dot(halves[b, g], k_s[b, :, cols])
             if g < 2:
                 query_grad = jnp.where(low, query_grad[0:112], query_grad[112:224])
             query_grad = query_grad * SCALING
-            key_grad = dot_tn(score_half, queries) * SCALING
-            value_grad = dot_tn(weights.astype(BF16), grads)
+            key_grad = dot(halves_t[b, g], q2s[b, g] if g < 2 else qr_s[b]) * SCALING
+            value_grad = dot(prob_t[b, g, :, 0:count].astype(BF16), grads[b, g])
             local[1, rows, cols] = value_grad.astype(BF16)
             if g < 2:
                 local[0, rows, cols] = query_grad.astype(BF16)
                 local[0, rows, 256 + 128 * g : 384 + 128 * g] = key_grad.astype(BF16)
             else:
                 local[0, rows, 512:640] = (query_grad + pltpu.roll(key_grad, 64, 1)).astype(BF16)
-        block = pl.ds(112 * b, 112)
-        core_copies.append(to_core(3 + b, local.at[1 - c, block], other.at[block]))
+    agt[c] = attention_grad.T
+    core_copies.append(to_core(2, local.at[1 - c], other))
+    core_copies.append(to_core(3, agt.at[c], agt.at[c]))
+    ad_copies = to_peers(7, lambda there: ad_a.at[x], lambda k: ad_a.at[x])
 
     def start_embeds():
         arrive(ad_copies)
@@ -487,7 +496,7 @@
     for p in TURNS:
         end(p, 1, flying[p, 1])
         flying[p, 2] = begin(p, 2)
-    for group, members in ((1, (2, 3)), (0, (0, 1)), (2, (4, 5))):
+    for group, members in ((1, (2, 3, 7, 8)), (0, (0, 1, 5, 6)), (2, (4, 9))):
         for p in members:
             end(p, 2, flying[p, 2])
         last_exchange(group)
@@ -504,7 +513,7 @@
         early, late = rows[0:20], rows[20:40]
         own_tiles.append(jnp.where(first_core, early, late))
         f_s[t, 0:20] = jnp.where(first_core, late, early).astype(BF16)
-    arrive([to_core(6, f_s, f_r)])
+    arrive([to_core(4, f_s, f_r)])
     for t in range(5):
         got = f_r[t, 0:20].astype(F32)
         left = jnp.where(first_core, own_tiles[t], got)
@@ -563,6 +572,8 @@
         vmem((336, 640), BF16),
         vmem((4, 5, 2, 160, 128), BF16),
         vmem((5, 160, 128), F32),
+        vmem((3, 3, 112, 224), F32),
+        vmem((3, 112, 160), BF16),
         vmem((4, 208, 128), BF16),
         vmem((3, 208, 128), BF16),
         vmem((5, 32, 128), BF16),
@@ -570,14 +581,14 @@
         dma((6,)),
         dma((9, 3)),
         dma((9, 3)),
-        dma((7,)),
-        dma((7,)),
-        dma((6, 3, 4)),
-        dma((6, 3, 4)),
+        dma((5,)),
+        dma((5,)),
+        dma((len(PARTS), 3, 4)),
+        dma((len(PARTS), 3, 4)),
         dma((3, 3)),
         dma((3, 3)),
     ]
-    assert len(scratch) == 46
+    assert len(scratch) == 48
     scratch += [vmem(received_shape(part, step), BF16) for part in PARTS for step in range(3)]
     in_vmem = pl.BlockSpec(memory_space=pltpu.VMEM)
     in_smem = pl.BlockSpec(memory_space=pltpu.SMEM)

time: 79 us -> 75.7 us (0.958)
  Pallas kernels: 77.5 us -> 74.3 us
    pallas_call x1, Pallas kernels: 75.8 us -> 72.5 us  [call(): pl.pallas_call(kernel, out_shape=(jax.ShapeDtypeStruct((40, 3584), BF16),...]
where the time goes in v4:
time: 75.7 us; the launch traced here: 75.6 us
  Pallas kernels  74.3 us (98%)
  between operations  1.29 us (2%)
    pallas_call x1, Pallas kernels, call(): pl.pallas_call(kernel, out_shape=(jax.ShapeDtypeStruct((40, 3584), BF16),...  72.5 us
    pallas_call x1, Pallas kernels, results(): pl.pallas_call(write_out, out_shape=tuple((jax.ShapeDtypeStruct(part.shap...  1.78 us

profile of v4, /device:TPU:1, one launch (start us, length us, event | category | flops | bytes accessed | tf_op | source)
XLA Modules:
  0.0 75.6 jit_solution(12448144357510828391)
XLA Ops:
  1.3 72.5 %sublayer.1 = (bf16[40,3584]{1,0:T(8,128)(2,1)}, f32[3,20,320]{2,1,0:T(8,128)}, f32[20,320]{1,0:T(8,128)}) custom-call(s32[1]{0:T(128)S(6)} %copy.11.refs_0_, s32[3]{0:T(128)} %refs_1_.1, s32[3,50]{1,0:T(4,128)} %refs_2_.1, bf16[3,100,320]{2,1,0:T(8,128)(2,1)} %refs_3_.1, bf16[40,3584]{1,0:T(8,128)(2,1)} %refs_4_.1, bf16[3,320,1280]{2,1,0:T(8,128)(2,1)} %bitcast.2, ...), custom_call_target="tpu_custom_call" | custom-call | tf_op jit(solution)/shard_map/sublayer/pallas_call | solution.py:596
  73.8 1.8 %results.1 = (bf16[40,3584]{1,0:T(8,128)(2,1)}, f32[3,20,320]{2,1,0:T(8,128)}, f32[20,320]{1,0:T(8,128)}) custom-call(bf16[40,3584]{1,0:T(8,128)(2,1)} %get-tuple-element.9.refs_0_, f32[3,20,320]{2,1,0:T(8,128)} %get-tuple-element.10.refs_1_, f32[20,320]{1,0:T(8,128)} %get-tuple-element.11.refs_2_), custom_call_target="tpu_custom_call" | custom-call | tf_op jit(solution)/shard_map/results/pallas_call | solution.py:620

commit v5 on v4

--- a/solution.py
+++ b/solution.py
@@ -12,11 +12,12 @@
 SCALING = 0.125
 PARTS = tuple(
     (tile, row, 80, order)
-    for row, orders in ((0, ("ABa", "BAb", "aAB", "bBA", "ABa")), (80, ("ABa", "BAb", "aAB", "bBA", "BAb")))
-    for tile, order in enumerate(orders)
+    for tile, orders in ((0, ("AaB", "BbA")), (1, ("aAB", "bBA")), (4, ("AaB", "BbA")), (2, ("AaB", "BbA")), (3, ("aAB", "bBA")))
+    for row, order in zip((0, 80), orders)
 )
-TURNS = (2, 3, 0, 1, 4, 7, 8, 5, 6, 9)
-Z_GROUPS = (((0, 1), 0, 80), ((2, 3), 80, 80), ((4,), 160, 48))
+WAVES = ((0, 1, 2, 3, 4, 5), (6, 7, 8, 9))
+Z_GROUPS = (((0, 1, 4), 0, 128), ((2, 3), 128, 80))
+TILE_ROWS = {0: 0, 1: 40, 4: 80, 2: 128, 3: 168}
 
 
 def dot(a, b):
@@ -175,17 +176,28 @@
         started.append(copy)
         return copy
 
+    def leave(copies):
+        for copy in copies:
+            copy.wait_send()
+            started[:] = [other_copy for other_copy in started if other_copy is not copy]
+
     def arrive(copies):
         for copy in copies:
             copy.wait_recv()
 
     audio_copies = []
     cot_copies = to_peers(3, lambda there: cot_s.at[there], lambda k: cot_r.at[x])
-    for b in range(3):
-        if b > 0:
-            pack_audio(b)
+
+    def send_audio(b):
         block = aud.at[x, b]
         audio_copies.append(to_peers(b, lambda there: block, lambda k: block))
+
+    send_audio(0)
+    pack_audio(1)
+    pack_audio(2)
+    leave(cot_copies)
+    send_audio(1)
+    send_audio(2)
 
     pos_pad = jnp.concatenate([positions[...].astype(F32), jnp.zeros((13, 50), F32)], axis=0).astype(BF16)
     frame_row = lax.broadcasted_iota(jnp.int32, (50, 112), 0)
@@ -268,17 +280,16 @@
             attp[g] = attp[g] + dot(placed, mixed.astype(BF16))
         return attp, pooled_audio
 
-    attp, pooled_audio = forward(0, attp, pooled_audio)
-
     weight_copies[2].wait()
     arrive(cot_copies)
     row_grads = jnp.concatenate([unfold(cot_r[s], 7) for s in range(4)], axis=0).astype(BF16)
     adapter_terms = dot_nt(row_grads, wp[...])
     for t in range(4):
         gt_s[t] = fold(adapter_terms[40 * t : 40 * t + 40], 640, 0)
+    attp, pooled_audio = forward(0, attp, pooled_audio)
+    leave(audio_copies[1] + audio_copies[2])
+    gt_copies = to_peers(4, lambda there: gt_s.at[there], lambda k: gt_r.at[k - 1])
     attp, pooled_audio = forward(1, attp, pooled_audio)
-    gt_copies = to_peers(4, lambda there: gt_s.at[there], lambda k: gt_r.at[k - 1])
-
     attp, pooled_audio = forward(2, attp, pooled_audio)
     attp = [part.astype(BF16) for part in attp]
     for g in range(2):
@@ -462,15 +473,14 @@
             store(3, out_part[:, 128:256])
             store(4, value_part[:, 256:384] + out_part[:, 256:384])
 
-        for p, part in enumerate(PARTS):
-            slots = {"A": (0, 1, None, None), "B": (0, None, 1, None)}.get(part[3][0], (0, 1, 2, 3))
+        for p in WAVES[0]:
+            slots = {"A": (0, 1, None, None), "B": (0, None, 1, None)}.get(PARTS[p][3][0], (0, 1, 2, 3))
             if slots[turn] is not None:
                 flying[p, 0] += begin(p, 0, slots[turn])
-    embed_copies = start_embeds()
     z_copies = []
 
-    def last_exchange(group):
-        tiles, first, count = Z_GROUPS[group]
+    def last_exchange(wave):
+        tiles, first, count = Z_GROUPS[wave]
         fill = count - 40 * len(tiles)
         for j in range(4):
             pieces = [final[t, 40 * j : 40 * j + 40] for t in tiles]
@@ -481,8 +491,8 @@
             copy = pltpu.make_async_remote_copy(
                 src_ref=z_s.at[zp ^ k, pl.ds(first, count)],
                 dst_ref=z_r.at[k - 1, pl.ds(first, count)],
-                send_sem=z_send.at[group, k - 1],
-                recv_sem=z_recv.at[group, k - 1],
+                send_sem=z_send.at[wave, k - 1],
+                recv_sem=z_recv.at[wave, k - 1],
                 device_id=z_peers[k - 1],
                 device_id_type=MESH,
             )
@@ -490,16 +500,25 @@
             z_copies.append(copy)
             started.append(copy)
 
-    for p in TURNS:
-        end(p, 0, flying[p, 0])
-        flying[p, 1] = begin(p, 1)
-    for p in TURNS:
-        end(p, 1, flying[p, 1])
-        flying[p, 2] = begin(p, 2)
-    for group, members in ((1, (2, 3, 7, 8)), (0, (0, 1, 5, 6)), (2, (4, 9))):
-        for p in members:
-            end(p, 2, flying[p, 2])
-        last_exchange(group)
+    def step(wave, number):
+        for p in WAVES[wave]:
+            end(p, number - 1, flying[p, number - 1])
+            if number < 3:
+                flying[p, number] = begin(p, number)
+
+    for p in WAVES[0]:
+        leave(flying[p, 0])
+    for p in WAVES[1]:
+        flying[p, 0] = begin(p, 0)
+    step(0, 1)
+    step(1, 1)
+    embed_copies = start_embeds()
+    step(0, 2)
+    step(1, 2)
+    step(0, 3)
+    last_exchange(0)
+    step(1, 3)
+    last_exchange(1)
     embeds_copy = finish_embeds(embed_copies)
     arrive(z_copies)
     mine = z_s[zp].astype(F32)
@@ -509,7 +528,7 @@
     own_tiles = []
     f_s[...] = jnp.zeros_like(f_s)
     for t in range(5):
-        rows = mine[40 * t : 40 * t + 40]
+        rows = mine[TILE_ROWS[t] : TILE_ROWS[t] + 40]
         early, late = rows[0:20], rows[20:40]
         own_tiles.append(jnp.where(first_core, early, late))
         f_s[t, 0:20] = jnp.where(first_core, late, early).astype(BF16)
@@ -585,8 +604,8 @@
         dma((5,)),
         dma((len(PARTS), 3, 4)),
         dma((len(PARTS), 3, 4)),
-        dma((3, 3)),
-        dma((3, 3)),
+        dma((2, 3)),
+        dma((2, 3)),
     ]
     assert len(scratch) == 48
     scratch += [vmem(received_shape(part, step), BF16) for part in PARTS for step in range(3)]

time: 75.7 us -> 72.8 us (0.962)
  Pallas kernels: 74.3 us -> 71.3 us
    pallas_call x1, Pallas kernels: 72.5 us -> 69.6 us  [call(): pl.pallas_call(kernel, out_shape=(jax.ShapeDtypeStruct((40, 3584), BF16),...]
where the time goes in v5:
time: 72.8 us; the launch traced here: 72.6 us
  Pallas kernels  71.3 us (98%)
  between operations  1.29 us (2%)
    pallas_call x1, Pallas kernels, call(): pl.pallas_call(kernel, out_shape=(jax.ShapeDtypeStruct((40, 3584), BF16),...  69.6 us
    pallas_call x1, Pallas kernels, results(): pl.pallas_call(write_out, out_shape=tuple((jax.ShapeDtypeStruct(part.shap...  1.78 us

profile of v5, /device:TPU:1, one launch (start us, length us, event | category | flops | bytes accessed | tf_op | source)
XLA Modules:
  0.0 72.6 jit_solution(16878553190903720465)
XLA Ops:
  1.3 69.6 %sublayer.1 = (bf16[40,3584]{1,0:T(8,128)(2,1)}, f32[3,20,320]{2,1,0:T(8,128)}, f32[20,320]{1,0:T(8,128)}) custom-call(s32[1]{0:T(128)S(6)} %copy.11.refs_0_, s32[3]{0:T(128)} %refs_1_.1, s32[3,50]{1,0:T(4,128)} %refs_2_.1, bf16[3,100,320]{2,1,0:T(8,128)(2,1)} %refs_3_.1, bf16[40,3584]{1,0:T(8,128)(2,1)} %refs_4_.1, bf16[3,320,1280]{2,1,0:T(8,128)(2,1)} %bitcast.2, ...), custom_call_target="tpu_custom_call" | custom-call | tf_op jit(solution)/shard_map/sublayer/pallas_call | solution.py:615
  70.8 1.8 %results.1 = (bf16[40,3584]{1,0:T(8,128)(2,1)}, f32[3,20,320]{2,1,0:T(8,128)}, f32[20,320]{1,0:T(8,128)}) custom-call(bf16[40,3584]{1,0:T(8,128)(2,1)} %get-tuple-element.9.refs_0_, f32[3,20,320]{2,1,0:T(8,128)} %get-tuple-element.10.refs_1_, f32[20,320]{1,0:T(8,128)} %get-tuple-element.11.refs_2_), custom_call_target="tpu_custom_call" | custom-call | tf_op jit(solution)/shard_map/results/pallas_call | solution.py:639

commit v6 on v5

--- a/solution.py
+++ b/solution.py
@@ -10,12 +10,21 @@
 BF16 = jnp.bfloat16
 EPSILON = 1e-05
 SCALING = 0.125
-PARTS = tuple(
-    (tile, row, 80, order)
-    for tile, orders in ((0, ("AaB", "BbA")), (1, ("aAB", "bBA")), (4, ("AaB", "BbA")), (2, ("AaB", "BbA")), (3, ("aAB", "bBA")))
-    for row, order in zip((0, 80), orders)
+PARTS = (
+    (0, 0, 80, "AaB"),
+    (0, 80, 80, "BbA"),
+    (1, 0, 80, "aAB"),
+    (1, 80, 80, "bBA"),
+    (4, 0, 48, "AaB"),
+    (4, 48, 48, "BbA"),
+    (4, 96, 32, "aAB"),
+    (4, 128, 32, "bBA"),
+    (2, 0, 80, "AaB"),
+    (2, 80, 80, "BbA"),
+    (3, 0, 80, "aAB"),
+    (3, 80, 80, "bBA"),
 )
-WAVES = ((0, 1, 2, 3, 4, 5), (6, 7, 8, 9))
+WAVES = ((0, 1, 2, 3, 4, 5, 6, 7), (8, 9, 10, 11))
 Z_GROUPS = (((0, 1, 4), 0, 128), ((2, 3), 128, 80))
 TILE_ROWS = {0: 0, 1: 40, 4: 80, 2: 128, 3: 168}
 
@@ -112,7 +121,6 @@
 
     lane = lax.broadcasted_iota(jnp.int32, (112, 128), 1)
     low = lane < 64
-    low_half = low[0:64]
     tmp[...] = jnp.zeros_like(tmp)
     pj[...] = jnp.zeros_like(pj)
     mgp[...] = jnp.zeros_like(mgp)
@@ -125,16 +133,20 @@
 
     def pack_audio(b):
         tmp[b, 0:100, 0:320] = aud_v[b].astype(F32)
-        first, second, third = (tmp[b, :, 128 * i : 128 * i + 128] for i in range(3))
+        first, second, third = (tmp[b, 0:104, 128 * i : 128 * i + 128] for i in range(3))
         second_turned = pltpu.roll(second, 64, 1)
-        packed = third[0:64] + pltpu.roll(third[64:128], 64, 1)
-        packed_odd = jnp.where(low_half, first[0:64], pltpu.roll(first[64:128], 64, 1))
-        even = jnp.concatenate([first[0:112], second[0:112], packed], axis=0)
+        blank = jnp.zeros((8, 128), F32)
+        even_low = jnp.concatenate([third[56:104], blank], axis=0)
+        odd_low = jnp.concatenate([first[56:104], blank], axis=0)
+        packed = third[0:56] + pltpu.roll(even_low, 64, 1)
+        packed_odd = jnp.where(low[0:56], first[0:56], pltpu.roll(odd_low, 64, 1))
+        even = jnp.concatenate([first, second, packed, blank], axis=0)
         odd = jnp.concatenate(
             [
-                jnp.where(low, pltpu.roll(first, 64, 1)[0:112], second_turned[0:112]),
-                jnp.where(low, second_turned[0:112], pltpu.roll(third, 64, 1)[0:112]),
+                jnp.where(low[0:104], pltpu.roll(first, 64, 1), second_turned),
+                jnp.where(low[0:104], second_turned, pltpu.roll(third, 64, 1)),
                 packed_odd,
+                blank,
             ],
             axis=0,
         )
@@ -146,9 +158,9 @@
     pl.semaphore_wait(barrier, len(everyone))
 
     started = []
-    def to_peers(slot, source, target):
+    def to_peers(slot, source, target, steps=(1, 2, 3)):
         copies = []
-        for k in (1, 2, 3):
+        for k in steps:
             there = (x + k) % 4
             copy = pltpu.make_async_remote_copy(
                 src_ref=source(there),
@@ -185,12 +197,21 @@
         for copy in copies:
             copy.wait_recv()
 
-    audio_copies = []
+    audio_copies, passed = [], []
     cot_copies = to_peers(3, lambda there: cot_s.at[there], lambda k: cot_r.at[x])
 
     def send_audio(b):
         block = aud.at[x, b]
-        audio_copies.append(to_peers(b, lambda there: block, lambda k: block))
+        audio_copies.append(to_peers(b, lambda there: block, lambda k: block, (1, 3)))
+
+    def pass_audio(b):
+        arrive(audio_copies[b])
+        top = aud.at[(x + 3) % 4, b, pl.ds(0, 144)]
+        bottom = aud.at[(x + 1) % 4, b, pl.ds(144, 128)]
+        passed.append(
+            to_peers(9 + b, lambda there: top, lambda k: top, (1,))
+            + to_peers(9 + b, lambda there: bottom, lambda k: bottom, (3,))
+        )
 
     send_audio(0)
     pack_audio(1)
@@ -231,18 +252,17 @@
     pooled_audio = jnp.zeros((40, 1280), F32)
 
     def forward(b, attp, pooled_audio):
-        arrive(audio_copies[b])
+        arrive(passed[b])
         tiles = []
         for s in (0, 2):
-            left = aud[s, b, 224:288].astype(F32)
-            right = aud[s + 1, b, 224:288].astype(F32)
-            top = jnp.where(low_half, left, pltpu.roll(right, 64, 1))
-            bottom = jnp.where(low_half, pltpu.roll(left, 64, 1), right)
-            tiles.append(aud[s, b, 0:112].astype(F32))
-            tiles.append(aud[s, b, 112:224].astype(F32))
-            tiles.append(jnp.concatenate([top, bottom[0:48]], axis=0))
-            tiles.append(aud[s + 1, b, 0:112].astype(F32))
-            tiles.append(aud[s + 1, b, 112:224].astype(F32))
+            left = aud[s, b].astype(F32)
+            right = aud[s + 1, b].astype(F32)
+            left_rest, right_rest = left[208:264], right[208:264]
+            top = jnp.where(low[0:56], left_rest, pltpu.roll(right_rest, 64, 1))
+            bottom = jnp.where(low[0:56], pltpu.roll(left_rest, 64, 1), right_rest)
+            middle = jnp.concatenate([top, bottom[0:48]], axis=0)
+            for tile in (left[0:104], left[104:208], middle, right[0:104], right[104:208]):
+                tiles.append(jnp.concatenate([tile, jnp.zeros((8, 128), F32)], axis=0))
         frames = jnp.concatenate(tiles, axis=1)
         pooled_audio = pooled_audio + dot(place(b, 40 * x, 40), frames.astype(BF16))
         normed = normalize(frames)[0].astype(BF16)
@@ -281,13 +301,16 @@
         return attp, pooled_audio
 
     weight_copies[2].wait()
+    pass_audio(0)
     arrive(cot_copies)
     row_grads = jnp.concatenate([unfold(cot_r[s], 7) for s in range(4)], axis=0).astype(BF16)
     adapter_terms = dot_nt(row_grads, wp[...])
     for t in range(4):
         gt_s[t] = fold(adapter_terms[40 * t : 40 * t + 40], 640, 0)
+    pass_audio(1)
+    pass_audio(2)
     attp, pooled_audio = forward(0, attp, pooled_audio)
-    leave(audio_copies[1] + audio_copies[2])
+    leave(passed[1] + passed[2])
     gt_copies = to_peers(4, lambda there: gt_s.at[there], lambda k: gt_r.at[k - 1])
     attp, pooled_audio = forward(1, attp, pooled_audio)
     attp, pooled_audio = forward(2, attp, pooled_audio)
@@ -562,7 +585,7 @@
         vmem((320, 1280), BF16),
         vmem((1280, 896), BF16),
         vmem((3, 128, 384), F32),
-        vmem((4, 3, 288, 128), BF16),
+        vmem((4, 3, 272, 128), BF16),
         vmem((4, 288, 128), BF16),
         vmem((4, 288, 128), BF16),
         vmem((4, 80, 640), BF16),
@@ -598,8 +621,8 @@
         vmem((5, 32, 128), BF16),
         vmem((5, 32, 128), BF16),
         dma((6,)),
-        dma((9, 3)),
-        dma((9, 3)),
+        dma((12, 3)),
+        dma((12, 3)),
         dma((5,)),
         dma((5,)),
         dma((len(PARTS), 3, 4)),

time: 72.8 us -> 77.8 us (1.069)
  Pallas kernels: 71.3 us -> 76.4 us
    pallas_call x1, Pallas kernels: 69.6 us -> 74.6 us  [call(): pl.pallas_call(kernel, out_shape=(jax.ShapeDtypeStruct((40, 3584), BF16),...]
where the time goes in v6:
time: 77.8 us; the launch traced here: 77.6 us
  Pallas kernels  76.4 us (98%)
  between operations  1.29 us (2%)
    pallas_call x1, Pallas kernels, call(): pl.pallas_call(kernel, out_shape=(jax.ShapeDtypeStruct((40, 3584), BF16),...  74.6 us
    pallas_call x1, Pallas kernels, results(): pl.pallas_call(write_out, out_shape=tuple((jax.ShapeDtypeStruct(part.shap...  1.78 us

profile of v6, /device:TPU:1, one launch (start us, length us, event | category | flops | bytes accessed | tf_op | source)
XLA Modules:
  0.0 77.6 jit_solution(4422733751316432388)
XLA Ops:
  1.3 74.6 %sublayer.1 = (bf16[40,3584]{1,0:T(8,128)(2,1)}, f32[3,20,320]{2,1,0:T(8,128)}, f32[20,320]{1,0:T(8,128)}) custom-call(s32[1]{0:T(128)S(6)} %copy.11.refs_0_, s32[3]{0:T(128)} %refs_1_.1, s32[3,50]{1,0:T(4,128)} %refs_2_.1, bf16[3,100,320]{2,1,0:T(8,128)(2,1)} %refs_3_.1, bf16[40,3584]{1,0:T(8,128)(2,1)} %refs_4_.1, bf16[3,320,1280]{2,1,0:T(8,128)(2,1)} %bitcast.2, ...), custom_call_target="tpu_custom_call" | custom-call | tf_op jit(solution)/shard_map/sublayer/pallas_call | solution.py:638
  75.9 1.8 %results.1 = (bf16[40,3584]{1,0:T(8,128)(2,1)}, f32[3,20,320]{2,1,0:T(8,128)}, f32[20,320]{1,0:T(8,128)}) custom-call(bf16[40,3584]{1,0:T(8,128)(2,1)} %get-tuple-element.9.refs_0_, f32[3,20,320]{2,1,0:T(8,128)} %get-tuple-element.10.refs_1_, f32[20,320]{1,0:T(8,128)} %get-tuple-element.11.refs_2_), custom_call_target="tpu_custom_call" | custom-call | tf_op jit(solution)/shard_map/results/pallas_call | solution.py:662

commit v7 on v6

--- a/solution.py
+++ b/solution.py
@@ -11,20 +11,14 @@
 EPSILON = 1e-05
 SCALING = 0.125
 PARTS = (
-    (0, 0, 80, "AaB"),
-    (0, 80, 80, "BbA"),
-    (1, 0, 80, "aAB"),
-    (1, 80, 80, "bBA"),
-    (4, 0, 48, "AaB"),
-    (4, 48, 48, "BbA"),
-    (4, 96, 32, "aAB"),
-    (4, 128, 32, "bBA"),
-    (2, 0, 80, "AaB"),
-    (2, 80, 80, "BbA"),
-    (3, 0, 80, "aAB"),
-    (3, 80, 80, "bBA"),
+    (0, 0, 160, "ABa"),
+    (1, 0, 160, "BAb"),
+    (4, 0, 80, "AaB"),
+    (4, 80, 80, "BbA"),
+    (2, 0, 160, "aAB"),
+    (3, 0, 160, "bBA"),
 )
-WAVES = ((0, 1, 2, 3, 4, 5, 6, 7), (8, 9, 10, 11))
+WAVES = ((0, 1, 2, 3, 4, 5), ())
 Z_GROUPS = (((0, 1, 4), 0, 128), ((2, 3), 128, 80))
 TILE_ROWS = {0: 0, 1: 40, 4: 80, 2: 128, 3: 168}
 
@@ -158,9 +152,9 @@
     pl.semaphore_wait(barrier, len(everyone))
 
     started = []
-    def to_peers(slot, source, target, steps=(1, 2, 3)):
+    def to_peers(slot, source, target):
         copies = []
-        for k in steps:
+        for k in (1, 2, 3):
             there = (x + k) % 4
             copy = pltpu.make_async_remote_copy(
                 src_ref=source(there),
@@ -197,21 +191,12 @@
         for copy in copies:
             copy.wait_recv()
 
-    audio_copies, passed = [], []
+    audio_copies = []
     cot_copies = to_peers(3, lambda there: cot_s.at[there], lambda k: cot_r.at[x])
 
     def send_audio(b):
         block = aud.at[x, b]
-        audio_copies.append(to_peers(b, lambda there: block, lambda k: block, (1, 3)))
-
-    def pass_audio(b):
-        arrive(audio_copies[b])
-        top = aud.at[(x + 3) % 4, b, pl.ds(0, 144)]
-        bottom = aud.at[(x + 1) % 4, b, pl.ds(144, 128)]
-        passed.append(
-            to_peers(9 + b, lambda there: top, lambda k: top, (1,))
-            + to_peers(9 + b, lambda there: bottom, lambda k: bottom, (3,))
-        )
+        audio_copies.append(to_peers(b, lambda there: block, lambda k: block))
 
     send_audio(0)
     pack_audio(1)
@@ -252,7 +237,7 @@
     pooled_audio = jnp.zeros((40, 1280), F32)
 
     def forward(b, attp, pooled_audio):
-        arrive(passed[b])
+        arrive(audio_copies[b])
         tiles = []
         for s in (0, 2):
             left = aud[s, b].astype(F32)
@@ -301,16 +286,13 @@
         return attp, pooled_audio
 
     weight_copies[2].wait()
-    pass_audio(0)
     arrive(cot_copies)
     row_grads = jnp.concatenate([unfold(cot_r[s], 7) for s in range(4)], axis=0).astype(BF16)
     adapter_terms = dot_nt(row_grads, wp[...])
     for t in range(4):
         gt_s[t] = fold(adapter_terms[40 * t : 40 * t + 40], 640, 0)
-    pass_audio(1)
-    pass_audio(2)
     attp, pooled_audio = forward(0, attp, pooled_audio)
-    leave(passed[1] + passed[2])
+    leave(audio_copies[1] + audio_copies[2])
     gt_copies = to_peers(4, lambda there: gt_s.at[there], lambda k: gt_r.at[k - 1])
     attp, pooled_audio = forward(1, attp, pooled_audio)
     attp, pooled_audio = forward(2, attp, pooled_audio)
@@ -529,15 +511,13 @@
             if number < 3:
                 flying[p, number] = begin(p, number)
 
-    for p in WAVES[0]:
-        leave(flying[p, 0])
     for p in WAVES[1]:
         flying[p, 0] = begin(p, 0)
     step(0, 1)
     step(1, 1)
-    embed_copies = start_embeds()
     step(0, 2)
     step(1, 2)
+    embed_copies = start_embeds()
     step(0, 3)
     last_exchange(0)
     step(1, 3)
@@ -621,8 +601,8 @@
         vmem((5, 32, 128), BF16),
         vmem((5, 32, 128), BF16),
         dma((6,)),
-        dma((12, 3)),
-        dma((12, 3)),
+        dma((9, 3)),
+        dma((9, 3)),
         dma((5,)),
         dma((5,)),
         dma((len(PARTS), 3, 4)),

time: 77.8 us -> 72.2 us (0.928)
  Pallas kernels: 76.4 us -> 70.7 us
    pallas_call x1, Pallas kernels: 74.6 us -> 69 us  [call(): pl.pallas_call(kernel, out_shape=(jax.ShapeDtypeStruct((40, 3584), BF16),...]
where the time goes in v7:
time: 72.2 us; the launch traced here: 72 us
  Pallas kernels  70.7 us (98%)
  between operations  1.29 us (2%)
    pallas_call x1, Pallas kernels, call(): pl.pallas_call(kernel, out_shape=(jax.ShapeDtypeStruct((40, 3584), BF16),...  69 us
    pallas_call x1, Pallas kernels, results(): pl.pallas_call(write_out, out_shape=tuple((jax.ShapeDtypeStruct(part.shap...  1.78 us

profile of v7, /device:TPU:1, one launch (start us, length us, event | category | flops | bytes accessed | tf_op | source)
XLA Modules:
  0.0 72.0 jit_solution(8862724979490442361)
XLA Ops:
  1.3 69.0 %sublayer.1 = (bf16[40,3584]{1,0:T(8,128)(2,1)}, f32[3,20,320]{2,1,0:T(8,128)}, f32[20,320]{1,0:T(8,128)}) custom-call(s32[1]{0:T(128)S(6)} %copy.11.refs_0_, s32[3]{0:T(128)} %refs_1_.1, s32[3,50]{1,0:T(4,128)} %refs_2_.1, bf16[3,100,320]{2,1,0:T(8,128)(2,1)} %refs_3_.1, bf16[40,3584]{1,0:T(8,128)(2,1)} %refs_4_.1, bf16[3,320,1280]{2,1,0:T(8,128)(2,1)} %bitcast.2, ...), custom_call_target="tpu_custom_call" | custom-call | tf_op jit(solution)/shard_map/sublayer/pallas_call | solution.py:618
  70.2 1.8 %results.1 = (bf16[40,3584]{1,0:T(8,128)(2,1)}, f32[3,20,320]{2,1,0:T(8,128)}, f32[20,320]{1,0:T(8,128)}) custom-call(bf16[40,3584]{1,0:T(8,128)(2,1)} %get-tuple-element.9.refs_0_, f32[3,20,320]{2,1,0:T(8,128)} %get-tuple-element.10.refs_1_, f32[20,320]{1,0:T(8,128)} %get-tuple-element.11.refs_2_), custom_call_target="tpu_custom_call" | custom-call | tf_op jit(solution)/shard_map/results/pallas_call | solution.py:642

commit v8 on v7

--- a/solution.py
+++ b/solution.py
@@ -633,17 +633,28 @@
 
 
 def write_out(*refs):
-    for source, target in zip(refs[:3], refs[3:]):
-        target[...] = source[...]
+    sources, targets, held, sems = refs[:3], refs[3:6], refs[6:9], refs[9]
+    arriving = [pltpu.make_async_copy(sources[i], held[i], sems.at[0, i]) for i in range(3)]
+    leaving = [pltpu.make_async_copy(held[i], targets[i], sems.at[1, i]) for i in range(3)]
+    for copy in arriving:
+        copy.start()
+    for i in (1, 2, 0):
+        arriving[i].wait()
+        leaving[i].start()
+    for copy in leaving:
+        copy.wait()
 
 
 def results(*parts):
-    in_vmem = pl.BlockSpec(memory_space=pltpu.VMEM)
+    anywhere = pl.BlockSpec(memory_space=pl.ANY)
     return pl.pallas_call(
         write_out,
         out_shape=tuple(jax.ShapeDtypeStruct(part.shape, part.dtype) for part in parts),
-        in_specs=[in_vmem] * 3,
-        out_specs=(in_vmem,) * 3,
+        in_specs=[anywhere] * 3,
+        out_specs=(anywhere,) * 3,
+        scratch_shapes=[pltpu.VMEM(part.shape, part.dtype) for part in parts]
+        + [pltpu.SemaphoreType.DMA((2, 3))],
+        compiler_params=pltpu.CompilerParams(vmem_limit_bytes=60 * 2**20),
         name="results",
     )(*parts)
 

time: 72.2 us -> 72.2 us (level)
  no operation moved by 1% of the time
where the time goes in v8:
time: 72.2 us; the launch traced here: 72 us
  Pallas kernels  70.8 us (98%)
  between operations  1.29 us (2%)
    pallas_call x1, Pallas kernels, call(): pl.pallas_call(kernel, out_shape=(jax.ShapeDtypeStruct((40, 3584), BF16),...  69 us
    pallas_call x1, Pallas kernels, results(): pl.pallas_call(write_out, out_shape=tuple((jax.ShapeDtypeStruct(part.shap...  1.8 us

profile of v8, /device:TPU:1, one launch (start us, length us, event | category | flops | bytes accessed | tf_op | source)
XLA Modules:
  0.0 72.0 jit_solution(3870791167841768083)
XLA Ops:
  1.3 69.0 %sublayer.1 = (bf16[40,3584]{1,0:T(8,128)(2,1)}, f32[3,20,320]{2,1,0:T(8,128)}, f32[20,320]{1,0:T(8,128)}) custom-call(s32[1]{0:T(128)S(6)} %copy.11.refs_0_, s32[3]{0:T(128)} %refs_1_.1, s32[3,50]{1,0:T(4,128)} %refs_2_.1, bf16[3,100,320]{2,1,0:T(8,128)(2,1)} %refs_3_.1, bf16[40,3584]{1,0:T(8,128)(2,1)} %refs_4_.1, bf16[3,320,1280]{2,1,0:T(8,128)(2,1)} %bitcast.2, ...), custom_call_target="tpu_custom_call" | custom-call | tf_op jit(solution)/shard_map/sublayer/pallas_call | solution.py:618
  70.2 1.8 %results.1 = (bf16[40,3584]{1,0:T(8,128)(2,1)}, f32[3,20,320]{2,1,0:T(8,128)}, f32[20,320]{1,0:T(8,128)}) custom-call(bf16[40,3584]{1,0:T(8,128)(2,1)} %get-tuple-element.9.refs_0_, f32[3,20,320]{2,1,0:T(8,128)} %get-tuple-element.10.refs_1_, f32[20,320]{1,0:T(8,128)} %get-tuple-element.11.refs_2_), custom_call_target="tpu_custom_call" | custom-call | tf_op jit(solution)/shard_map/results/pallas_call | solution.py:650
